TPU v7x, 32 devices: a whole 2x2x4 slice. The times are simulated.
32 devices in a mesh: wide: 8 (over z, y), narrow: 4 (over x, core).
Axes of the slice: x: 2, y: 2, z: 4, core: 2. Of those that a mesh axis runs over, the one named last changes fastest.
Arguments:
- tables_in: bfloat16 [8192, 768], P(('wide', 'narrow')), may hold values from -6 to 6
- cotangent: bfloat16 [8192, 768], P(('wide', 'narrow')), may hold values from -6 to 6
- cell_ids: int32 [32, 256], P(('wide', 'narrow')), may hold values from 0 to 241, as said below
- lengths: int32 [32], P(('wide', 'narrow')), may hold values from 64 to 256
- qkv_weight: bfloat16 [2, 768, 2304], P(None, 'narrow'), may hold values from -0.21875 to 0.21875
- q_bias: bfloat16 [2, 768], P(None, 'narrow'), may hold values from -3 to 3
- v_bias: bfloat16 [2, 768], P(None, 'narrow'), may hold values from -3 to 3
- o_weight: bfloat16 [2, 768, 768], P(None, 'narrow'), may hold values from -0.875 to 0.875
- o_bias: bfloat16 [2, 768], P(None, 'narrow'), may hold values from -2 to 2
- norm1_gain: bfloat16 [2, 768], P(None, 'narrow'), may hold values from 0.5 to 1.5
- norm1_bias: bfloat16 [2, 768], P(None, 'narrow'), may hold values from -2 to 2
- in_weight: bfloat16 [2, 768, 3072], P(None, 'narrow'), may hold values from -0.21875 to 0.21875
- in_bias: bfloat16 [2, 3072], P(None, 'narrow'), may hold values from -3 to 3
- out_weight: bfloat16 [2, 3072, 768], P(None, 'narrow'), may hold values from -0.109375 to 0.109375
- out_bias: bfloat16 [2, 768], P(None, 'narrow'), may hold values from -2 to 2
- norm2_gain: bfloat16 [2, 768], P(None, 'narrow'), may hold values from 0.5 to 1.5
- norm2_bias: bfloat16 [2, 768], P(None, 'narrow'), may hold values from -2 to 2
Outputs:
- mixed_out: bfloat16 [8192, 768], P(('wide', 'narrow'))
- input_grad: bfloat16 [8192, 768], P(('wide', 'narrow'))
- qkv_grad: float32 [2, 768, 2304], P(None, 'narrow')
- q_bias_grad: float32 [2, 768], P(None, 'narrow')
- v_bias_grad: float32 [2, 768], P(None, 'narrow')
- o_weight_grad: float32 [2, 768, 768], P(None, 'narrow')
- o_bias_grad: float32 [2, 768], P(None, 'narrow')
- norm1_gain_grad: float32 [2, 768], P(None, 'narrow')
- norm1_bias_grad: float32 [2, 768], P(None, 'narrow')
- in_weight_grad: float32 [2, 768, 3072], P(None, 'narrow')
- in_bias_grad: float32 [2, 3072], P(None, 'narrow')
- out_weight_grad: float32 [2, 3072, 768], P(None, 'narrow')
- out_bias_grad: float32 [2, 768], P(None, 'narrow')
- norm2_gain_grad: float32 [2, 768], P(None, 'narrow')
- norm2_bias_grad: float32 [2, 768], P(None, 'narrow')
Inputs may be any that keep to these rules, and one draw needn't show every extreme that they name: `cell_ids`: along a table the ids never fall; id 0 marks the question tokens at the table's head, never fewer than 16 of them; every other id marks one cell of that table.
All inputs are finite; a program needn't handle non-finite values.
Results may differ from a plain program's by a relative error of at most 0.023.
Values may be sent and summed in bfloat16 or wider, within the bound.
No kernel may reach another device: no remote copies, remote signals or barrier semaphores. Data moves between devices by JAX's collectives and lax.ppermute only.
A program may use at most 320 MiB of HBM per device.

v0:
```python
import functools
import math

import jax
import jax.numpy as jnp
from jax import lax
from jax.experimental import pallas as pl
from jax.experimental.pallas import tpu as pltpu
from jax.sharding import PartitionSpec as P

HEADS = 12
norm_eps = 1e-12
masked_score = -1000000000.0
low = jnp.bfloat16
f32 = jnp.float32
VMEM_BYTES = 56 * 1024 * 1024
HALVINGS = 2


def swap(value, axis, bit):
    count = lax.axis_size(axis)
    return lax.ppermute(value, axis, [(i, i ^ bit) for i in range(count)])


def dot(a, b):
    return jnp.dot(a, b, preferred_element_type=f32)


def dot_nt(a, b):
    return lax.dot_general(a, b, (((1,), (1,)), ((), ())), preferred_element_type=f32)


def dot_tn(a, b):
    return lax.dot_general(a, b, (((0,), (0,)), ((), ())), preferred_element_type=f32)


def normalize(residual):
    center = residual - jnp.mean(residual, axis=-1, keepdims=True)
    inverse = lax.rsqrt(jnp.mean(center * center, axis=-1, keepdims=True) + norm_eps)
    return center * inverse, inverse


def normalize_back(grad_unit, unit, inverse):
    centered = grad_unit - jnp.mean(grad_unit, axis=-1, keepdims=True)
    return inverse * (centered - unit * jnp.mean(grad_unit * unit, axis=-1, keepdims=True))


def weight_copies(ids, layer, pieces, target, columns, sems, base):
    own, core, near_x, far_x, diagonal = pieces
    rows = own.shape[1]
    half = rows // 2
    n, y = ids[0], ids[4]
    copies = []

    def add(source, start, count):
        where = target.at[pl.ds(pl.multiple_of(start, half), count), :]
        copies.append(pltpu.make_async_copy(source, where, sems.at[base + len(copies)]))

    at = pl.ds(columns, target.shape[1])
    add(own.at[layer], n * rows, rows)
    add(core.at[layer], ids[1] * rows, rows)
    add(near_x.at[:, at], ids[2] * rows + y * half, half)
    add(far_x.at[:, at], ids[2] * rows + (1 - y) * half, half)
    add(diagonal.at[pl.ds(0, half), at], ids[3] * rows + y * half, half)
    add(diagonal.at[pl.ds(half, half), at], ids[3] * rows + (1 - y) * half, half)
    return copies


def begin(copies):
    for copy in copies:
        copy.start()


def finish(copies):
    for copy in copies:
        copy.wait()


def attn_copies(layer, ids, refs, w_qkv, w_o, sems):
    qkv_own, qkv_core, o_own, o_core = refs[:4]
    halves = refs[4:]
    qkv = weight_copies(ids, layer, (qkv_own, qkv_core) + halves, w_qkv, 0, sems, 0)
    o = weight_copies(ids, layer, (o_own, o_core) + halves, w_o, w_qkv.shape[1], sems, 6)
    return qkv, o


def ffn_copies(layer, ids, refs, w_in, w_out, sems):
    in_copies = weight_copies(ids, layer, refs[:5], w_in, 0, sems, 0)
    out_copies = weight_copies(ids, layer, refs[5:], w_out, 0, sems, 6)
    return in_copies, out_copies


def pack_kernel(*refs):
    shorts, in_bias, packed = refs[:8], refs[8], refs[9]
    layers, share = shorts[0].shape
    for layer in range(layers):
        for i, short in enumerate(shorts):
            packed[layer, i : i + 1, :] = short[layer : layer + 1, :].astype(f32)
        for i in range(4):
            packed[layer, 8 + i : 9 + i, :] = in_bias[layer : layer + 1, i * share : (i + 1) * share].astype(f32)


def attn_fwd_kernel(layer, ids, length, x, cell_row, small, *rest):
    weights, rest = rest[:7], rest[7:]
    qkv_rows, probs, context, unit_out, inverse_out, w_qkv, w_o, mask, sems = rest
    tokens, width = x.shape
    qkv_copies, o_copies = attn_copies(layer, ids, weights, w_qkv, w_o, sems)
    begin(qkv_copies)
    begin(o_copies)
    position = lax.broadcasted_iota(jnp.int32, (1, tokens), 1)
    key_cell = cell_row[...]
    square = (tokens, tokens)
    diagonal = lax.broadcasted_iota(jnp.int32, square, 0) == lax.broadcasted_iota(jnp.int32, square, 1)
    query_cell = jnp.sum(jnp.where(diagonal, key_cell, 0), axis=1, keepdims=True)
    allowed = (query_cell == key_cell) | (key_cell == 0) | (query_cell == 0)
    allowed = allowed & (position < length[0])
    mask[...] = jnp.where(allowed, 0.0, masked_score)
    scale = 1.0 / math.sqrt(width // HEADS)
    finish(qkv_copies)
    tile = width // 2

    for t in range(6):
        columns = slice(t * tile, (t + 1) * tile)
        rows = dot(x[...], w_qkv[:, columns])
        if t // 2 != 1:
            part = slice((t % 2) * tile, (t % 2 + 1) * tile)
            rows = rows + small[layer, t // 4 : t // 4 + 1, part]
        if t < 2:
            rows = rows * scale
        qkv_rows[:, columns] = rows.astype(low)

    pair_width = 2 * width // HEADS
    first = lax.broadcasted_iota(jnp.int32, (1, pair_width), 1) < pair_width // 2

    for pair in range(HEADS // 2):
        at = slice(pair * pair_width, (pair + 1) * pair_width)
        query = qkv_rows[:, at]
        key = qkv_rows[:, width + at.start : width + at.stop]
        value = qkv_rows[:, 2 * width + at.start : 2 * width + at.stop]
        sides = []
        for side in range(2):
            mine = first if side == 0 else jnp.logical_not(first)
            scores = dot_nt(jnp.where(mine, query, jnp.zeros_like(query)), key) + mask[...]
            shifted = jnp.exp(scores - jnp.max(scores, axis=-1, keepdims=True))
            total = jnp.sum(shifted, axis=-1, keepdims=True)
            prob = (shifted * (1.0 / total)).astype(low)
            probs[2 * pair + side] = prob
            sides.append(dot(prob, value))
        context[:, at] = jnp.where(first, sides[0], sides[1]).astype(low)

    finish(o_copies)
    residual = x[...].astype(f32) + (dot(context[...], w_o[...]) + small[layer, 2:3, :])
    unit, inverse = normalize(residual)
    unit_out[...] = unit
    inverse_out[...] = inverse


def gelu_and_slope(x):
    t = 1.0 / (1.0 + (0.3275911 * math.sqrt(0.5)) * jnp.abs(x))
    bell = jnp.exp(-0.5 * x * x)
    series = 1.421413741 + t * (-1.453152027 + t * 1.061405429)
    series = t * (0.254829592 + t * (-0.284496736 + t * series))
    tail = 0.5 * series * bell
    cdf = jnp.where(x >= 0.0, 1.0 - tail, tail)
    return (x * cdf).astype(low), cdf + x * (bell * (1.0 / math.sqrt(2.0 * math.pi)))


def ffn_fwd_kernel(layer, ids, unit_one, in_bias, small, *rest):
    weights, rest = rest[:10], rest[10:]
    hidden_out, slope_out, unit_out, inverse_out, result = rest[:5]
    w_in, w_out, normed_low, hidden, slope, sems, out_sems = rest[5:]
    in_copies, out_copies = ffn_copies(layer, ids, weights, w_in, w_out, sems)
    begin(in_copies)
    begin(out_copies)
    normed = unit_one[...] * small[layer, 3:4, :] + small[layer, 4:5, :]
    normed_low[...] = normed.astype(low)
    finish(in_copies)
    tile = w_in.shape[1] // 8
    going = []
    for t in range(8):
        columns = pl.ds(t * tile, tile)
        pre = dot(normed_low[...], w_in[:, columns]) + in_bias[layer, :, columns]
        hidden[:, columns], slope[:, columns] = gelu_and_slope(pre)
        leaving = [
            pltpu.make_async_copy(hidden.at[:, columns], hidden_out.at[:, columns], out_sems.at[2 * t]),
            pltpu.make_async_copy(slope.at[:, columns], slope_out.at[:, columns], out_sems.at[2 * t + 1]),
        ]
        begin(leaving)
        going += leaving

    finish(out_copies)
    residual = unit_one[...] * small[layer, 3:4, :] + small[layer, 4:5, :] + (dot(hidden[...], w_out[...]) + small[layer, 5:6, :])
    unit, inverse = normalize(residual)
    unit_out[...] = unit
    inverse_out[...] = inverse
    result[...] = (unit * small[layer, 6:7, :] + small[layer, 7:8, :]).astype(low)
    finish(going)


WIDE_BIT = {"y": 0, "z": 1}


def place_of(ids, owner, piece, way):
    away = None if owner is None else ids[0] ^ owner
    off = None if piece is None else piece ^ ids[5]
    place = [None if away is None else away & 1]
    for name in way:
        if name == "x":
            place.append(pl.ds(0, 2) if away is None else away >> 1)
        else:
            place.append(pl.ds(0, 2) if off is None else (off >> WIDE_BIT[name]) & 1)
    return tuple(place) + (pl.ds(0, 2) if piece is None else piece >> 2,)


def store_rows(stage, ids, product, piece, way):
    share = product.shape[0] // 4
    for owner in range(4):
        block = product[owner * share : (owner + 1) * share].astype(low)
        stage[place_of(ids, owner, piece, way) + (pl.ds(0, share),)] = block


def piece_copies(stage, ids, piece, way, kept, sent, sems, turn):
    at = place_of(ids, None, piece, way)[1:]
    copies = [
        pltpu.make_async_copy(stage.at[(1,) + at], sent.at[at], sems.at[2 * turn]),
        pltpu.make_async_copy(stage.at[(0,) + at], kept.at[at], sems.at[2 * turn + 1]),
    ]
    begin(copies)
    return copies


def out_bwd_kernel(layer, way, ids, grad, unit_two, inverse_two, hidden, small, *rest):
    d_ffn, d_resid_two, small_grads, kept, sent, stage, out_sems = rest
    g = grad[...].astype(f32)
    unit = unit_two[...]
    small_grads[0:1, :] = jnp.sum(g * unit, axis=0, keepdims=True)
    small_grads[1:2, :] = jnp.sum(g, axis=0, keepdims=True)
    d_two = normalize_back(g * small[layer, 6:7, :], unit, inverse_two[...])
    d_resid_two[...] = d_two
    d_low = d_two.astype(low)
    d_ffn[...] = d_low
    small_grads[2:3, :] = jnp.sum(d_low.astype(f32), axis=0, keepdims=True)
    small_grads[3:8, :] = jnp.zeros((5, unit.shape[1]), f32)
    tile = hidden.shape[1] // 8
    share = d_ffn.shape[1] // 4
    waits = []
    for owner in range(4):
        for half in range(2):
            columns = slice((2 * owner + half) * tile, (2 * owner + half + 1) * tile)
            out_grad = dot_tn(hidden[:, columns], d_ffn[...])
            for row_group in range(2):
                for column_group in range(2):
                    piece = (half * 2 + row_group) * 2 + column_group
                    block = out_grad[
                        row_group * share : (row_group + 1) * share,
                        column_group * tile : (column_group + 1) * tile,
                    ]
                    stage[place_of(ids, owner, piece, way)] = block.astype(low)
        core, *at = place_of(ids, owner, None, way)
        at = tuple(at)
        to_kept = pltpu.make_async_copy(stage.at[(0,) + at], kept.at[at], out_sems.at[owner])
        to_sent = pltpu.make_async_copy(stage.at[(1,) + at], sent.at[at], out_sems.at[owner])
        pl.when(core == 0)(to_kept.start)
        pl.when(core == 1)(to_sent.start)
        waits.append(to_kept)
    finish(waits)


def in_bwd_kernel(layer, way, ids, d_ffn, d_resid_two, unit_one, inverse_one, small, slope_in, *rest):
    weights, rest = rest[:10], rest[10:]
    d_resid, small_grads, in_bias_grad, kept, sent = rest[:5]
    w_in, w_out, d_pre, normed_t, slope, stage, sems, out_sems, slope_sem = rest[5:]
    in_copies, out_copies = ffn_copies(layer, ids, weights, w_in, w_out, sems)
    slope_copy = pltpu.make_async_copy(slope_in, slope, slope_sem.at[0])
    begin(out_copies[:2] + [slope_copy] + out_copies[2:] + in_copies)
    normed = unit_one[...] * small[layer, 3:4, :] + small[layer, 4:5, :]
    normed_t[...] = normed.astype(low).T
    tile = w_in.shape[1] // 8
    going = []
    slope_copy.wait()
    for turn in range(8):
        if turn % 2 == 0:
            finish(([out_copies[0]], [out_copies[1]], out_copies[2:4], out_copies[4:6])[turn // 2])
        t = 2 * ids[turn // 2] + turn % 2
        columns = pl.ds(pl.multiple_of(t * tile, tile), tile)
        d_hidden = dot_nt(d_ffn[...], w_out[columns, :])
        d_tile = (d_hidden * slope[:, columns]).astype(low)
        d_pre[:, columns] = d_tile
        in_bias_grad[:, columns] = jnp.sum(d_tile.astype(f32), axis=0, keepdims=True)
        store_rows(stage, ids, dot(normed_t[...], d_tile), t, way)
        going += piece_copies(stage, ids, t, way, kept, sent, out_sems, turn)
    finish(in_copies)
    d_normed = d_resid_two[...] + dot_nt(d_pre[...], w_in[...])
    unit = unit_one[...]
    small_grads[0:1, :] = jnp.sum(d_normed * unit, axis=0, keepdims=True)
    small_grads[1:2, :] = jnp.sum(d_normed, axis=0, keepdims=True)
    small_grads[2:8, :] = jnp.zeros((6, unit.shape[1]), f32)
    d_resid[...] = normalize_back(d_normed * small[layer, 3:4, :], unit, inverse_one[...])
    finish(going)


def attn_bwd_kernel(layer, way, ids, d_resid, x, qkv_rows, probs, context, *rest):
    weights, others, rest = rest[:7], rest[7:-13], rest[-13:]
    d_input, small_grads, kept, sent = rest[:4]
    w_qkv, w_o, d_attn, d_context, d_qkv, x_t, stage, sems, out_sems = rest[4:]
    tokens, width = x.shape
    qkv_copies, o_copies = attn_copies(layer, ids, weights, w_qkv, w_o, sems)
    begin(o_copies)
    begin(qkv_copies)
    d_low = d_resid[...].astype(low)
    d_attn[...] = d_low
    small_grads[2:3, :] = jnp.sum(d_low.astype(f32), axis=0, keepdims=True)
    x_t[...] = x[...].T
    tile = width // 2
    for half in range(2):
        product = dot_tn(context[...], d_attn[:, half * tile : (half + 1) * tile])
        store_rows(stage, ids, product, 6 + half, way)
    finish(o_copies)
    d_context[...] = dot_nt(d_attn[...], w_o[...]).astype(low)
    pair_width = 2 * width // HEADS
    first = lax.broadcasted_iota(jnp.int32, (1, pair_width), 1) < pair_width // 2
    scale = 1.0 / math.sqrt(width // HEADS)

    for pair in range(HEADS // 2):
        at_query = slice(pair * pair_width, (pair + 1) * pair_width)
        at_key = slice(width + at_query.start, width + at_query.stop)
        at_value = slice(2 * width + at_query.start, 2 * width + at_query.stop)
        query, key, value = qkv_rows[:, at_query], qkv_rows[:, at_key], qkv_rows[:, at_value]
        d_ctx = d_context[:, at_query]
        sides = []
        for side in range(2):
            mine = first if side == 0 else jnp.logical_not(first)
            prob_low = probs[2 * pair + side]
            prob = prob_low.astype(f32)
            d_prob = dot_nt(jnp.where(mine, d_ctx, jnp.zeros_like(d_ctx)), value)
            inner = jnp.sum(prob * d_prob, axis=-1, keepdims=True)
            d_scores = (prob * (d_prob - inner)).astype(low)
            sides.append((dot(d_scores, key), dot_tn(d_scores, query), dot_tn(prob_low, d_ctx)))
        d_qkv[:, at_query] = (jnp.where(first, sides[0][0], sides[1][0]) * scale).astype(low)
        d_qkv[:, at_key] = jnp.where(first, sides[0][1], sides[1][1]).astype(low)
        d_qkv[:, at_value] = jnp.where(first, sides[0][2], sides[1][2]).astype(low)

    small_grads[0:1, :] = jnp.sum(d_qkv[:, :width].astype(f32), axis=0, keepdims=True)
    small_grads[1:2, :] = jnp.sum(d_qkv[:, 2 * width :].astype(f32), axis=0, keepdims=True)
    small_grads[3:8, :] = jnp.zeros((5, width), f32)
    if others:
        share = width // 4
        sources = small_sources(layer, small_grads, others)
        for owner in range(4):
            for piece in range(8):
                lines = []
                for source, row, start, step in sources[3 * piece : 3 * piece + 3]:
                    line = source[row : row + 1, start + owner * step : start + owner * step + share]
                    lines.append(jnp.concatenate([line, jnp.zeros_like(line)], axis=1))
                lines.append(jnp.zeros((SMALL_ROWS - 3, tile), f32))
                block = jnp.concatenate(lines, axis=0).astype(low)
                stage[place_of(ids, owner, piece, way) + (pl.ds(share, SMALL_ROWS),)] = block
    going = []
    for piece in (6, 7, 0, 1, 2, 3, 4, 5):
        if piece < 6:
            store_rows(stage, ids, dot(x_t[...], d_qkv[:, piece * tile : (piece + 1) * tile]), piece, way)
        going += piece_copies(stage, ids, piece, way, kept, sent, out_sems, piece)
    finish(qkv_copies)
    d_input[...] = (d_resid[...] + dot_nt(d_qkv[...], w_qkv[...])).astype(low)
    finish(going)


SMALL_ROWS = 16
SMALL_LINES = (("attn", 0), ("attn", 1), ("attn", 2), ("in", 0), ("in", 1), ("out", 2), ("out", 0), ("out", 1))


def small_sources(layer, own, others):
    found = []
    out_0, in_0, bias_0, out_1, in_1, bias_1, attn_1 = others
    refs = ({"attn": own, "in": in_0, "out": out_0}, {"attn": attn_1, "in": in_1, "out": out_1})
    width = own.shape[1]
    for of_layer, bias in zip(refs, (bias_0, bias_1)):
        found += [(of_layer[name], row, 0, width // 4) for name, row in SMALL_LINES]
        found += [(bias, 0, i * (width // 4), width) for i in range(4)]
    return found


def unpack_kernel(layer, slab, back, earlier, ids, near, far, *rest):
    outs = rest[earlier:-4]
    buffer, wide_buffer, in_sems, out_sems = rest[-4:]
    share, tile = wide_buffer.shape[1:]

    def fetch(piece, ref, index):
        return pltpu.make_async_copy(ref.at[index], buffer.at[piece], in_sems.at[piece])

    for piece in range(8):
        off = piece ^ ids[5]
        inner, outer = [(off >> WIDE_BIT[name]) & 1 for name in back]
        pl.when(outer == 0)(fetch(piece, near, (inner, piece >> 2)).start)
        pl.when(outer == 1)(fetch(piece, far, (inner, piece >> 2)).start)

    copies = []
    for piece in range(8):
        fetch(piece, near, (0, 0)).wait()
        wide_buffer[piece] = buffer[piece, :share].astype(f32)
        columns = pl.ds(piece * tile, tile)
        if slab == "in":
            target = outs[0].at[layer, :, columns]
        elif slab == "out":
            rows = pl.ds((piece // 2) * share, share)
            target = outs[0].at[layer, rows, pl.ds((piece % 2) * tile, tile)]
        elif piece < 6:
            target = outs[0].at[layer, :, columns]
        else:
            target = outs[1].at[layer, :, pl.ds((piece - 6) * tile, tile)]
        copies.append(pltpu.make_async_copy(wide_buffer.at[piece], target, out_sems.at[piece]))
        copies[-1].start()
    if slab == "attn" and layer == 0:
        for line in range(24):
            of_layer, which = line // 12, line % 12
            row = share + line % 3
            values = buffer[line // 3, row : row + 1, :share].astype(f32)
            if which < 8:
                outs[2 + which][of_layer : of_layer + 1, :] = values
            else:
                at = (which - 8) * share
                outs[10][of_layer : of_layer + 1, at : at + share] = values
    else:
        outs[-1][...] = jnp.zeros(outs[-1].shape, f32)
    finish(copies)


SMEM = pl.BlockSpec(memory_space=pltpu.SMEM)
VMEM = pl.BlockSpec(memory_space=pltpu.VMEM)
ANY = pl.BlockSpec(memory_space=pl.ANY)


def call(kernel, name, time, in_specs, out_specs, out_shape, scratch, args, aliases=()):
    return pl.pallas_call(
        kernel,
        name=name,
        in_specs=in_specs,
        out_specs=out_specs,
        out_shape=out_shape,
        scratch_shapes=scratch,
        input_output_aliases=dict(aliases),
        compiler_params=pltpu.CompilerParams(vmem_limit_bytes=VMEM_BYTES),
        cost_estimate=pl.CostEstimate(
            flops=int(time * 0.22e9), bytes_accessed=int(time * 0.72e6), transcendentals=0
        ),
    )(*args)


def shape(dims, kind):
    return jax.ShapeDtypeStruct(dims, kind)


def added(a, b):
    return (a.astype(f32) + b.astype(f32)).astype(low)


WAYS = ("xyz", "zxy", "yxz", "xzy", "xyz", "xyz")
BACKS = ("zy", "zy", "zy", "zy", "yz", "zy")
PLAN = (
    "out1", "in1", 0, 1, "attn1", "out0", 0, 2, 1, 3, 0, 1, 0, "in0", 2, 0, 4, 1, 0, 3, "attn0", 0, 2, 1, 5,
    3, 2, 4, 1, 3, 4, 2, 5, 4, 3, 1, 2, 5, 3, 4, 5, 2, 3, 5, 4, 5, 4, 5,
)


class Order:
    def __init__(self):
        self.last = None

    def after(self, values):
        if self.last is None:
            return values
        values, self.last = lax.optimization_barrier((values, self.last))
        return values

    def wait(self, values):
        values = self.after(values)
        self.last = values
        return values


STEPS = {"x": ("narrow", 2), "y": ("wide", 1), "z": ("wide", 2)}


class Slab:
    def __init__(self, way, back, wide_count, kept, sent):
        self.kept = kept
        self.way, self.back = way, back
        self.rest = [1 << b for b in range(HALVINGS, wide_count.bit_length() - 1)]
        self.flying = swap(sent, "narrow", 1)
        self.stage = 0

    def step(self, order):
        received = order.after(self.flying)
        stage, way = self.stage, self.way
        if stage < len(way):
            send = added(self.kept[1], received[1])
            self.kept = added(self.kept[0], received[0])
            self.flying = swap(send, *STEPS[way[stage]])
            order.last = send
        elif stage < len(way) + 1 + len(self.back):
            if stage == len(way):
                piece = added(self.kept, received)
                if not self.rest:
                    self.block = piece[None]
            elif stage == len(way) + 1 and self.rest:
                piece = added(self.kept, received)
                for bit in self.rest[1:]:
                    piece = added(piece, swap(piece, "wide", bit))
                self.block = piece[None]
            else:
                self.block = jnp.concatenate([self.block, received], axis=0)
                piece = self.block
            order.last = piece
            if stage == len(way) and self.rest:
                self.kept = piece
                self.flying = swap(piece, "wide", self.rest[0])
            else:
                self.flying = swap(self.block, *STEPS[self.back[stage - len(way) - 1]])
        else:
            self.far = received
        self.stage += 1

    def ended(self):
        return self.stage == len(self.way) + len(self.back) + 2


def body(
    tables_in,
    cotangent,
    cell_ids,
    lengths,
    qkv_weight,
    q_bias,
    v_bias,
    o_weight,
    o_bias,
    norm1_gain,
    norm1_bias,
    in_weight,
    in_bias,
    out_weight,
    out_bias,
    norm2_gain,
    norm2_bias,
):
    tokens, width = tables_in.shape
    layers, share, ffn = in_weight.shape
    ffn_share = out_weight.shape[1]
    wide_count = lax.axis_size("wide")
    assert wide_count & (wide_count - 1) == 0 and wide_count >= 1 << HALVINGS and lax.axis_size("narrow") == 4
    tile = ffn // 8
    me = lax.axis_index("narrow").astype(jnp.int32)
    wide_me = lax.axis_index("wide").astype(jnp.int32)
    y = wide_me & 1
    ids = jnp.stack([me, me ^ 1, me ^ 2, me ^ 3, y, wide_me & (2**HALVINGS - 1)])

    order = Order()

    def half_of(weight, layer):
        rows = weight.shape[1] // 2
        return lax.dynamic_slice(weight, (layer, y * rows, 0), (1, rows, weight.shape[2]))[0]

    halves = []
    for layer in range(layers):
        joint = jnp.concatenate([half_of(qkv_weight, layer), half_of(o_weight, layer)], axis=1)
        halves += [joint, half_of(in_weight, layer), half_of(out_weight, layer)]
    near_x, far_x, diagonal = [None] * len(halves), [None] * len(halves), [None] * len(halves)
    core = [None] * 4
    own = (qkv_weight, o_weight, in_weight, out_weight)

    def group(i):
        return near_x[i], far_x[i], diagonal[i]

    def attn_weights(layer):
        return (qkv_weight, core[0], o_weight, core[1]) + group(3 * layer)

    def ffn_weights(layer):
        return (in_weight, core[2]) + group(3 * layer + 1) + (out_weight, core[3]) + group(3 * layer + 2)

    def in_order(low_one, high_one, bit):
        swapped = (me & bit) != 0
        return jnp.stack([jnp.where(swapped, high_one, low_one), jnp.where(swapped, low_one, high_one)])

    near_x[0] = swap(halves[0], "narrow", 2)
    order.last = halves[0]
    core[0], core[1] = swap(own[0], "narrow", 1), swap(own[1], "narrow", 1)
    short = order.after((q_bias, v_bias, o_bias, norm1_gain, norm1_bias, out_bias, norm2_gain, norm2_bias))
    packed = call(
        pack_kernel, "pack", 1, [VMEM] * 9, VMEM, shape((layers, 12, share), f32), [], tuple(short) + (in_bias,)
    )
    halves[1:], packed = order.wait((halves[1:], packed))
    near_x[0], core[0], core[1] = order.wait((near_x[0], core[0], core[1]))

    others = [
        lax.ppermute(order.after(packed), "narrow", [(i, i ^ away) for i in range(4)]) for away in (1, 2, 3)
    ]
    far_x[0] = swap(near_x[0], "wide", 1)
    near_x[1] = swap(order.after(halves[1]), "narrow", 2)
    far_x[0], near_x[1], others = order.wait((far_x[0], near_x[1], others))
    packed = in_order(in_order(packed, others[0], 1), in_order(others[1], others[2], 1), 2)
    packed = packed.reshape(4, layers, 12, share)
    small = packed[:, :, :8].transpose(1, 2, 0, 3).reshape(layers, 8, width)
    full_in_bias = packed[:, :, 8:].transpose(1, 0, 2, 3).reshape(layers, 1, ffn)

    def join(i):
        both = jnp.concatenate([near_x[i], far_x[i]], axis=0)
        diagonal[i] = swap(both, "narrow", 1)
        return both

    def begin_round(i):
        both = join(i)
        if i + 1 < len(halves):
            far_x[i + 1] = swap(near_x[i + 1], "wide", 1)
        if i + 2 < len(halves):
            near_x[i + 2] = swap(order.after(halves[i + 2]), "narrow", 2)
        order.last = both

    def end_round(i):
        if i + 2 < len(halves):
            far_x[i + 1], near_x[i + 2] = order.wait((far_x[i + 1], near_x[i + 2]))
        elif i + 1 < len(halves):
            far_x[i + 1] = order.wait(far_x[i + 1])

    def arrive(i):
        diagonal[i] = order.wait(diagonal[i])

    begin_round(0)
    core[2], core[3] = swap(order.after(own[2]), "narrow", 1), swap(order.after(own[3]), "narrow", 1)
    ids, small, full_in_bias = order.wait((ids, small, full_in_bias))
    arrive(0)
    core[2], core[3] = order.wait((core[2], core[3]))
    end_round(0)

    w_qkv = pltpu.VMEM((width, 3 * width), low)
    w_o = pltpu.VMEM((width, width), low)
    w_in = pltpu.VMEM((width, ffn), low)
    w_out = pltpu.VMEM((ffn, width), low)
    copy_sems = pltpu.SemaphoreType.DMA((12,))
    piece_sems = pltpu.SemaphoreType.DMA((16,))
    rows_f32 = shape((tokens, width), f32)
    rows_low = shape((tokens, width), low)
    column_f32 = shape((tokens, 1), f32)
    eight_f32 = shape((8, width), f32)

    def pieces(rows):
        return [shape((2, 2, 2, 2, rows, tile), low)] * 2

    def stage(rows):
        return pltpu.VMEM((2, 2, 2, 2, 2, rows, tile), low)

    def attn_forward(layer, x):
        x = order.after(x)
        outs = call(
            functools.partial(attn_fwd_kernel, layer),
            "attn_fwd",
            13,
            [SMEM, SMEM] + [VMEM] * 3 + [ANY] * 7,
            [VMEM] * 5,
            [shape((tokens, 3 * width), low), shape((HEADS, tokens, tokens), low), rows_low, rows_f32, column_f32],
            [w_qkv, w_o, pltpu.VMEM((tokens, tokens), f32), copy_sems],
            (ids, lengths, x, cell_ids, small) + attn_weights(layer),
        )
        order.last = outs[-1]
        return outs

    def ffn_forward(layer, unit_one):
        unit_one = order.after(unit_one)
        outs = call(
            functools.partial(ffn_fwd_kernel, layer),
            "ffn_fwd",
            10,
            [SMEM] + [VMEM] * 3 + [ANY] * 10,
            [ANY] * 2 + [VMEM] * 3,
            [shape((tokens, ffn), low), shape((tokens, ffn), f32), rows_f32, column_f32, rows_low],
            [
                w_in,
                w_out,
                pltpu.VMEM((tokens, width), low),
                pltpu.VMEM((tokens, ffn), low),
                pltpu.VMEM((tokens, ffn), f32),
                copy_sems,
                piece_sems,
            ],
            (ids, unit_one, full_in_bias, small) + ffn_weights(layer),
        )
        order.last = outs[-2]
        return outs

    def out_backward(layer, way, grad, unit_two, inverse_two, hidden):
        grad = order.after(grad)
        outs = call(
            functools.partial(out_bwd_kernel, layer, way),
            "out_bwd",
            8,
            [SMEM] + [VMEM] * 5,
            [VMEM] * 3 + [ANY] * 2,
            [rows_low, rows_f32, eight_f32] + pieces(share),
            [stage(share), pltpu.SemaphoreType.DMA((4,))],
            (ids, grad, unit_two, inverse_two, hidden, small),
        )
        order.last = outs[2]
        return outs

    def in_backward(layer, way, d_ffn, d_resid_two, unit_one, inverse_one, slope):
        d_ffn = order.after(d_ffn)
        outs = call(
            functools.partial(in_bwd_kernel, layer, way),
            "in_bwd",
            14,
            [SMEM] + [VMEM] * 5 + [ANY] * 11,
            [VMEM] * 3 + [ANY] * 2,
            [rows_f32, eight_f32, shape((1, ffn), f32)] + pieces(share),
            [
                w_in,
                w_out,
                pltpu.VMEM((tokens, ffn), low),
                pltpu.VMEM((width, tokens), low),
                pltpu.VMEM((tokens, ffn), f32),
                stage(share),
                copy_sems,
                piece_sems,
                pltpu.SemaphoreType.DMA((1,)),
            ],
            (ids, d_ffn, d_resid_two, unit_one, inverse_one, small, slope) + ffn_weights(layer),
        )
        order.last = outs[1]
        return outs

    def attn_backward(layer, way, d_resid, x, qkv_rows, probs, context, small_others):
        d_resid = order.after(d_resid)
        rows = share + (SMALL_ROWS if small_others else 0)
        outs = call(
            functools.partial(attn_bwd_kernel, layer, way),
            "attn_bwd",
            16,
            [SMEM] + [VMEM] * 5 + [ANY] * 7 + [VMEM] * len(small_others),
            [VMEM] * 2 + [ANY] * 2,
            [rows_low, eight_f32] + pieces(rows),
            [
                w_qkv,
                w_o,
                pltpu.VMEM((tokens, width), low),
                pltpu.VMEM((tokens, width), low),
                pltpu.VMEM((tokens, 3 * width), low),
                pltpu.VMEM((width, tokens), low),
                stage(rows),
                copy_sems,
                piece_sems,
            ],
            (ids, d_resid, x, qkv_rows, probs, context) + attn_weights(layer) + tuple(small_others),
        )
        order.last = outs[1]
        return outs

    def unpack(layer, name, slab, earlier):
        dims = {
            "attn": [(layers, share, 3 * width), (layers, share, width)],
            "in": [(layers, share, ffn)],
            "out": [(layers, ffn_share, width)],
        }[name]
        last = name == "attn" and layer == 0
        extra = [(layers, share)] * 8 + [(layers, ffn_share)] if last else [(8, 128)]
        near, far = order.after((slab.block, slab.far))
        rows = near.shape[2]
        outs = call(
            functools.partial(unpack_kernel, layer, name, slab.back, len(earlier)),
            "unpack",
            4,
            [SMEM] + [ANY] * (2 + len(earlier)),
            [ANY] * len(dims) + [VMEM] * len(extra),
            [shape(d, f32) for d in dims + extra],
            [
                pltpu.VMEM((8, rows, tile), low),
                pltpu.VMEM((8, share, tile), f32),
                pltpu.SemaphoreType.DMA((8,)),
                pltpu.SemaphoreType.DMA((8,)),
            ],
            (ids, near, far, *earlier),
            {3 + i: i for i in range(len(earlier))},
        )
        order.last = outs[-1]
        return tuple(outs)

    begin_round(1)
    first_attn = attn_forward(0, tables_in)
    arrive(1)
    end_round(1)
    begin_round(2)
    arrive(2)
    first_ffn = ffn_forward(0, first_attn[3])
    end_round(2)
    begin_round(3)
    arrive(3)
    second_attn = attn_forward(1, first_ffn[4])
    end_round(3)
    begin_round(4)
    arrive(4)
    end_round(4)
    begin_round(5)
    arrive(5)
    second_ffn = ffn_forward(1, second_attn[3])
    mixed_out = second_ffn[4]
    inputs = (tables_in, first_ffn[4])
    attn_kept, ffn_kept = (first_attn, second_attn), (first_ffn, second_ffn)

    slabs = [None] * 6
    grad = cotangent
    small_out, small_in, small_attn, bias_grads = [None] * 2, [None] * 2, [None] * 2, [None] * 2
    unpacked = {"attn": (), "in": (), "out": ()}
    for action in PLAN:
        if isinstance(action, int):
            slab = slabs[action]
            slab.step(order)
            if slab.ended():
                name = ("out", "in", "attn")[action % 3]
                unpacked[name] = unpack(layers - 1 - action // 3, name, slab, unpacked[name][: 2 if name == "attn" else 1])
            continue
        name, layer = action[:-1], int(action[-1])
        which = 3 * (layers - 1 - layer) + ("out", "in", "attn").index(name)
        way = WAYS[which]
        qkv_rows, probs, context, unit_one, inverse_one = attn_kept[layer]
        hidden, slope, unit_two, inverse_two, _ = ffn_kept[layer]
        if name == "out":
            d_ffn, d_resid_two, small_out[layer], kept, sent = out_backward(
                layer, way, grad, unit_two, inverse_two, hidden
            )
        elif name == "in":
            d_resid, small_in[layer], bias_grads[layer], kept, sent = in_backward(
                layer, way, d_ffn, d_resid_two, unit_one, inverse_one, slope
            )
        else:
            small_others = ()
            if layer == 0:
                small_others = (
                    small_out[0],
                    small_in[0],
                    bias_grads[0],
                    small_out[1],
                    small_in[1],
                    bias_grads[1],
                    small_attn[1],
                )
            grad, small_attn[layer], kept, sent = attn_backward(
                layer, way, d_resid, inputs[layer], qkv_rows, probs, context, small_others
            )
        slabs[which] = Slab(way, BACKS[which], wide_count, kept, sent)
    qkv_grad, o_grad, *vectors = unpacked["attn"]
    in_grad, out_grad = unpacked["in"][0], unpacked["out"][0]
    return (
        mixed_out,
        grad,
        qkv_grad,
        vectors[0],
        vectors[1],
        o_grad,
        vectors[2],
        vectors[3],
        vectors[4],
        in_grad,
        vectors[8],
        out_grad,
        vectors[5],
        vectors[6],
        vectors[7],
    )


def solution(mesh):
    by_table = P(("wide", "narrow"), None)
    matrix = P(None, "narrow", None)
    vector = P(None, "narrow")
    return jax.shard_map(
        body,
        mesh=mesh,
        in_specs=(
            by_table,
            by_table,
            by_table,
            P(("wide", "narrow")),
            matrix,
            vector,
            vector,
            matrix,
            vector,
            vector,
            vector,
            matrix,
            vector,
            matrix,
            vector,
            vector,
            vector,
        ),
        out_specs=(
            by_table,
            by_table,
            matrix,
            vector,
            vector,
            matrix,
            vector,
            vector,
            vector,
            matrix,
            vector,
            matrix,
            vector,
            vector,
            vector,
        ),
        check_vma=False,
    )
```

profile of v0, /device:TPU:0, one launch (start us, length us, event | category | flops | bytes accessed | tf_op | source)
XLA Modules:
  0.0 479.2 jit_solution(4941882478594026865)
XLA Ops:
  4.3 2.9 collective-permute-start
  9.7 2.5 dynamic-slice_bitcast_fusion
  13.0 8.5 %collective-permute-done.rest_4_ = bf16[96,3072]{1,0:T(8,128)(2,1)S(1)} collective-permute-done((bf16[96,3072]{1,0:T(8,128)(2,1)}, bf16[96,3072]{1,0:T(8,128)(2,1)S(1)}, u32[]{:S(2)}, u32[]{:S(2)}) %collective-permute-start) | collective-permute-done | bytes 589856 | tf_op jit(solution)/shard_map/ppermute | solution.py:22
  21.6 2.1 collective-permute-start.3
  26.4 7.6 %collective-permute-done.7 = f32[2,12,192]{2,1,0:T(8,128)S(1)} collective-permute-done((f32[2,12,192]{2,1,0:T(8,128)S(1)}, f32[2,12,192]{2,1,0:T(8,128)S(1)}, u32[]{:S(2)}, u32[]{:S(2)}) %collective-permute-start.7) | collective-permute-done | bytes 18464 | tf_op jit(solution)/shard_map/ppermute | solution.py:595
  47.7 7.1 %collective-permute-done.9.rest_7_ = bf16[384,768]{1,0:T(8,128)(2,1)} collective-permute-done((bf16[384,768]{1,0:T(8,128)(2,1)}, bf16[384,768]{1,0:T(8,128)(2,1)}, u32[]{:S(2)}, u32[]{:S(2)}) %collective-permute-start.9) | collective-permute-done | bytes 589856 | tf_op jit(solution)/shard_map/ppermute | solution.py:22
  58.7 8.1 %attn_fwd.2 = (bf16[256,2304]{1,0:T(8,128)(2,1)}, bf16[12,256,256]{2,1,0:T(8,128)(2,1)}, bf16[256,768]{1,0:T(8,128)(2,1)}, f32[256,768]{1,0:T(8,128)}, f32[256,1]{1,0:T(8,128)}) custom-call(s32[6]{0:T(128)} %stack.50.ids, s32[1]{0:T(128)S(6)} %copy.53.length, bf16[256,768]{1,0:T(8,128)(2,1)} %x.2, s32[1,256]{1,0:T(1,128)} %cell_row.3, ...), custom_call_target="tpu_custom_call" | custom-call | flops 2860000000 | bytes 9360000 | tf_op jit(solution)/shard_map/attn_fwd/pallas_call | solution.py:434
  66.8 3.8 collective-permute-done.14.rest_4_
  76.0 10.6 %ffn_fwd.2 = (bf16[256,3072]{1,0:T(8,128)(2,1)}, f32[256,3072]{1,0:T(8,128)}, f32[256,768]{1,0:T(8,128)}, f32[256,1]{1,0:T(8,128)}, bf16[256,768]{1,0:T(8,128)(2,1)}) custom-call(s32[6]{0:T(128)} %stack.50.ids, f32[256,768]{1,0:T(8,128)} %get-tuple-element.225.unit_one, f32[2,1,3072]{2,1,0:T(1,128)} %reshape.387.in_bias, f32[2,8,768]{2,1,0:T(8,128)} %reshape.386.small, ...), custom_call_target="tpu_custom_call" | custom-call | flops 2200000000 | bytes 7200000 | tf_op jit(solution)/shard_map/ffn_fwd/pallas_call | solution.py:434
  92.2 8.0 %attn_fwd.3 = (bf16[256,2304]{1,0:T(8,128)(2,1)}, bf16[12,256,256]{2,1,0:T(8,128)(2,1)}, bf16[256,768]{1,0:T(8,128)(2,1)}, f32[256,768]{1,0:T(8,128)}, f32[256,1]{1,0:T(8,128)}) custom-call(s32[6]{0:T(128)} %stack.50.ids, s32[1]{0:T(128)S(6)} %copy.53.length, bf16[256,768]{1,0:T(8,128)(2,1)} %get-tuple-element.232.x, s32[1,256]{1,0:T(1,128)} %cell_row.3, ...), custom_call_target="tpu_custom_call" | custom-call | flops 2860000000 | bytes 9360000 | tf_op jit(solution)/shard_map/attn_fwd/pallas_call | solution.py:434
  100.2 4.6 collective-permute-done.21.rest_7_
  107.8 12.9 %collective-permute-done.22.rest_8_ = bf16[384,768]{1,0:T(8,128)(2,1)S(1)} collective-permute-done((bf16[384,768]{1,0:T(8,128)(2,1)S(1)}, bf16[384,768]{1,0:T(8,128)(2,1)S(1)}, u32[]{:S(2)}, u32[]{:S(2)}) %collective-permute-start.22) | collective-permute-done | bytes 589856 | tf_op jit(solution)/shard_map/ppermute | solution.py:22
  120.8 2.8 collective-permute-done.24.rest_9_
  124.7 10.6 %ffn_fwd.3 = (bf16[256,3072]{1,0:T(8,128)(2,1)}, f32[256,3072]{1,0:T(8,128)}, f32[256,768]{1,0:T(8,128)}, f32[256,1]{1,0:T(8,128)}, bf16[256,768]{1,0:T(8,128)(2,1)}) custom-call(s32[6]{0:T(128)} %stack.50.ids, f32[256,768]{1,0:T(8,128)} %get-tuple-element.242.unit_one, f32[2,1,3072]{2,1,0:T(1,128)} %reshape.387.in_bias, f32[2,8,768]{2,1,0:T(8,128)} %reshape.386.small, ...), custom_call_target="tpu_custom_call" | custom-call | flops 2200000000 | bytes 7200000 | tf_op jit(solution)/shard_map/ffn_fwd/pallas_call | solution.py:434
  135.3 6.1 %out_bwd.2 = (bf16[256,768]{1,0:T(8,128)(2,1)}, f32[256,768]{1,0:T(8,128)}, f32[8,768]{1,0:T(8,128)}, bf16[2,2,2,2,192,384]{5,4,3,2,1,0:T(8,128)(2,1)}, bf16[2,2,2,2,192,384]{5,4,3,2,1,0:T(8,128)(2,1)}) custom-call(s32[6]{0:T(128)} %stack.50.ids, bf16[256,768]{1,0:T(8,128)(2,1)} %grad, f32[256,768]{1,0:T(8,128)} %get-tuple-element.246.unit_two, ...), custom_call_target="tpu_custom_call" | custom-call | flops 1760000000 | bytes 5760000 | tf_op jit(solution)/shard_map/out_bwd/pallas_call | solution.py:434
  141.5 14.7 %in_bwd.2 = (f32[256,768]{1,0:T(8,128)}, f32[8,768]{1,0:T(8,128)}, f32[1,3072]{1,0:T(1,128)}, bf16[2,2,2,2,192,384]{5,4,3,2,1,0:T(8,128)(2,1)}, bf16[2,2,2,2,192,384]{5,4,3,2,1,0:T(8,128)(2,1)}) custom-call(s32[6]{0:T(128)} %stack.50.ids, bf16[256,768]{1,0:T(8,128)(2,1)} %get-tuple-element.250.d_ffn, f32[256,768]{1,0:T(8,128)} %get-tuple-element.251.d_resid_two, ...), custom_call_target="tpu_custom_call" | custom-call | flops 3080000000 | bytes 10080000 | tf_op jit(solution)/shard_map/in_bwd/pallas_call | solution.py:434
  157.5 3.7 collective-permute-done.25
  161.9 13.0 %attn_bwd.2 = (bf16[256,768]{1,0:T(8,128)(2,1)}, f32[8,768]{1,0:T(8,128)}, bf16[2,2,2,2,192,384]{5,4,3,2,1,0:T(8,128)(2,1)}, bf16[2,2,2,2,192,384]{5,4,3,2,1,0:T(8,128)(2,1)}) custom-call(s32[6]{0:T(128)} %stack.50.ids, f32[256,768]{1,0:T(8,128)} %get-tuple-element.261.d_resid, bf16[256,768]{1,0:T(8,128)(2,1)} %get-tuple-element.232.x, ...), custom_call_target="tpu_custom_call" | custom-call | flops 3520000000 | bytes 11520000 | tf_op jit(solution)/shard_map/attn_bwd/pallas_call | solution.py:434
  175.4 6.0 %out_bwd.3 = (bf16[256,768]{1,0:T(8,128)(2,1)}, f32[256,768]{1,0:T(8,128)}, f32[8,768]{1,0:T(8,128)}, bf16[2,2,2,2,192,384]{5,4,3,2,1,0:T(8,128)(2,1)}, bf16[2,2,2,2,192,384]{5,4,3,2,1,0:T(8,128)(2,1)}) custom-call(s32[6]{0:T(128)} %stack.50.ids, bf16[256,768]{1,0:T(8,128)(2,1)} %get-tuple-element.267.grad, f32[256,768]{1,0:T(8,128)} %get-tuple-element.268.unit_two, ...), custom_call_target="tpu_custom_call" | custom-call | flops 1760000000 | bytes 5760000 | tf_op jit(solution)/shard_map/out_bwd/pallas_call | solution.py:434
  184.5 25.4 %collective-permute-done.27 = bf16[2,2,2,192,384]{4,3,2,1,0:T(8,128)(2,1)S(1)} collective-permute-done((bf16[2,2,2,192,384]{4,3,2,1,0:T(8,128)(2,1)S(1)}, bf16[2,2,2,192,384]{4,3,2,1,0:T(8,128)(2,1)S(1)}, u32[]{:S(2)}, u32[]{:S(2)}) %collective-permute-start.27) | collective-permute-done | bytes 1179680 | tf_op jit(solution)/shard_map/ppermute | solution.py:22
  214.8 10.3 %collective-permute-done.28 = bf16[2,2,192,384]{3,2,1,0:T(8,128)(2,1)S(1)} collective-permute-done((bf16[2,2,192,384]{3,2,1,0:T(8,128)(2,1)S(1)}, bf16[2,2,192,384]{3,2,1,0:T(8,128)(2,1)S(1)}, u32[]{:S(2)}, u32[]{:S(2)}) %collective-permute-start.28) | collective-permute-done | bytes 589856 | tf_op jit(solution)/shard_map/ppermute | solution.py:22
  225.2 1.6 collective-permute-start.32
  227.6 5.4 %collective-permute-done.32 = bf16[2,192,384]{2,1,0:T(8,128)(2,1)S(1)} collective-permute-done((bf16[2,192,384]{2,1,0:T(8,128)(2,1)S(1)}, bf16[2,192,384]{2,1,0:T(8,128)(2,1)S(1)}, u32[]{:S(2)}, u32[]{:S(2)}) %collective-permute-start.32) | collective-permute-done | bytes 294944 | tf_op jit(solution)/shard_map/ppermute | solution.py:22
  233.0 14.8 %in_bwd.3 = (f32[256,768]{1,0:T(8,128)}, f32[8,768]{1,0:T(8,128)}, f32[1,3072]{1,0:T(1,128)}, bf16[2,2,2,2,192,384]{5,4,3,2,1,0:T(8,128)(2,1)}, bf16[2,2,2,2,192,384]{5,4,3,2,1,0:T(8,128)(2,1)}) custom-call(s32[6]{0:T(128)} %stack.50.ids, bf16[256,768]{1,0:T(8,128)(2,1)} %get-tuple-element.283.d_ffn, f32[256,768]{1,0:T(8,128)} %get-tuple-element.284.d_resid_two, ...), custom_call_target="tpu_custom_call" | custom-call | flops 3080000000 | bytes 10080000 | tf_op jit(solution)/shard_map/in_bwd/pallas_call | solution.py:434
  249.5 2.6 collective-permute-start.35
  253.7 23.1 %collective-permute-done.36 = bf16[2,2,2,192,384]{4,3,2,1,0:T(8,128)(2,1)S(1)} collective-permute-done((bf16[2,2,2,192,384]{4,3,2,1,0:T(8,128)(2,1)S(1)}, bf16[2,2,2,192,384]{4,3,2,1,0:T(8,128)(2,1)S(1)}, u32[]{:S(2)}, u32[]{:S(2)}) %collective-permute-start.36) | collective-permute-done | bytes 1179680 | tf_op jit(solution)/shard_map/ppermute | solution.py:22
  277.2 1.6 collective-permute-start.37
  279.5 3.2 collective-permute-done.38
  282.8 2.6 collective-permute-done.37
  285.8 12.9 %attn_bwd.3 = (bf16[256,768]{1,0:T(8,128)(2,1)}, f32[8,768]{1,0:T(8,128)}, bf16[2,2,2,2,208,384]{5,4,3,2,1,0:T(8,128)(2,1)}, bf16[2,2,2,2,208,384]{5,4,3,2,1,0:T(8,128)(2,1)}) custom-call(s32[6]{0:T(128)} %stack.50.ids, f32[256,768]{1,0:T(8,128)} %get-tuple-element.296.d_resid, bf16[256,768]{1,0:T(8,128)(2,1)} %x.2, ...), custom_call_target="tpu_custom_call" | custom-call | flops 3520000000 | bytes 11520000 | tf_op jit(solution)/shard_map/attn_bwd/pallas_call | solution.py:434
  299.9 2.5 collective-permute-start.41
  302.5 12.1 %collective-permute-done.42 = bf16[2,2,192,384]{3,2,1,0:T(8,128)(2,1)S(1)} collective-permute-done((bf16[2,2,192,384]{3,2,1,0:T(8,128)(2,1)S(1)}, bf16[2,2,192,384]{3,2,1,0:T(8,128)(2,1)S(1)}, u32[]{:S(2)}, u32[]{:S(2)}) %collective-permute-start.42) | collective-permute-done | bytes 589856 | tf_op jit(solution)/shard_map/ppermute | solution.py:22
  317.8 1.6 collective-permute-start.50
  319.5 2.3 fusion
  322.8 8.0 %collective-permute-done.45 = bf16[2,2,192,384]{3,2,1,0:T(8,128)(2,1)S(1)} collective-permute-done((bf16[2,2,192,384]{3,2,1,0:T(8,128)(2,1)S(1)}, bf16[2,2,192,384]{3,2,1,0:T(8,128)(2,1)S(1)}, u32[]{:S(2)}, u32[]{:S(2)}) %collective-permute-start.45) | collective-permute-done | bytes 589856 | tf_op jit(solution)/shard_map/ppermute | solution.py:22
  330.8 6.2 %collective-permute-done.44 = bf16[2,192,384]{2,1,0:T(8,128)(2,1)S(1)} collective-permute-done((bf16[2,192,384]{2,1,0:T(8,128)(2,1)S(1)}, bf16[2,192,384]{2,1,0:T(8,128)(2,1)S(1)}, u32[]{:S(2)}, u32[]{:S(2)}) %collective-permute-start.44) | collective-permute-done | bytes 294944 | tf_op jit(solution)/shard_map/ppermute | solution.py:22
  337.2 7.7 %collective-permute-done.47 = bf16[2,2,2,192,384]{4,3,2,1,0:T(8,128)(2,1)S(1)} collective-permute-done((bf16[2,2,2,192,384]{4,3,2,1,0:T(8,128)(2,1)S(1)}, bf16[2,2,2,192,384]{4,3,2,1,0:T(8,128)(2,1)S(1)}, u32[]{:S(2)}, u32[]{:S(2)}) %collective-permute-start.47) | collective-permute-done | bytes 1179680 | tf_op jit(solution)/shard_map/ppermute | solution.py:22
  345.2 1.6 collective-permute-start.48
  347.3 2.6 collective-permute-start.46
  350.0 13.7 %collective-permute-done.49 = bf16[2,192,384]{2,1,0:T(8,128)(2,1)S(1)} collective-permute-done((bf16[2,192,384]{2,1,0:T(8,128)(2,1)S(1)}, bf16[2,192,384]{2,1,0:T(8,128)(2,1)S(1)}, u32[]{:S(2)}, u32[]{:S(2)}) %collective-permute-start.49) | collective-permute-done | bytes 294944 | tf_op jit(solution)/shard_map/ppermute | solution.py:22
  366.2 2.6 collective-permute-start.56
  368.8 1.9 collective-permute-done.43
  371.0 1.6 collective-permute-start.51
  372.6 5.3 %collective-permute-done.52 = bf16[1,2,192,384]{3,2,1,0:T(8,128)(2,1)S(1)} collective-permute-done((bf16[1,2,192,384]{3,2,1,0:T(8,128)(2,1)S(1)}, bf16[1,2,192,384]{3,2,1,0:T(8,128)(2,1)S(1)}, u32[]{:S(2)}, u32[]{:S(2)}) %collective-permute-start.52) | collective-permute-done | bytes 294944 | tf_op jit(solution)/shard_map/ppermute | solution.py:22
  377.9 3.8 collective-permute-done.54
  381.9 3.3 collective-permute-start.57
  386.5 9.6 %collective-permute-done.57 = bf16[1,2,192,384]{3,2,1,0:T(8,128)(2,1)S(1)} collective-permute-done((bf16[1,2,192,384]{3,2,1,0:T(8,128)(2,1)S(1)}, bf16[1,2,192,384]{3,2,1,0:T(8,128)(2,1)S(1)}, u32[]{:S(2)}, u32[]{:S(2)}) %collective-permute-start.57) | collective-permute-done | bytes 294944 | tf_op jit(solution)/shard_map/ppermute | solution.py:22
  397.3 4.3 collective-permute-done.53
  401.7 2.3 collective-permute-start.58
  406.0 11.2 %collective-permute-done.58 = bf16[2,208,384]{2,1,0:T(8,128)(2,1)S(1)} collective-permute-done((bf16[2,208,384]{2,1,0:T(8,128)(2,1)S(1)}, bf16[2,208,384]{2,1,0:T(8,128)(2,1)S(1)}, u32[]{:S(2)}, u32[]{:S(2)}) %collective-permute-start.58) | collective-permute-done | bytes 319520 | tf_op jit(solution)/shard_map/ppermute | solution.py:22
  417.3 1.6 collective-permute-start.64
  419.4 6.1 %collective-permute-done.60 = bf16[1,2,192,384]{3,2,1,0:T(8,128)(2,1)S(1)} collective-permute-done((bf16[1,2,192,384]{3,2,1,0:T(8,128)(2,1)S(1)}, bf16[1,2,192,384]{3,2,1,0:T(8,128)(2,1)S(1)}, u32[]{:S(2)}, u32[]{:S(2)}) %collective-permute-start.60) | collective-permute-done | bytes 294944 | tf_op jit(solution)/shard_map/ppermute | solution.py:22
  425.5 1.6 collective-permute-start.65
  427.2 1.8 collective-permute-start.63
  430.0 3.7 unpack.10
  433.7 4.4 collective-permute-done.64.far
  439.0 3.7 unpack.8
  442.7 8.1 %collective-permute-done.62.far = bf16[2,2,192,384]{3,2,1,0:T(8,128)(2,1)S(1)} collective-permute-done((bf16[2,2,192,384]{3,2,1,0:T(8,128)(2,1)S(1)}, bf16[2,2,192,384]{3,2,1,0:T(8,128)(2,1)S(1)}, u32[]{:S(2)}, u32[]{:S(2)}) %collective-permute-start.62) | collective-permute-done | bytes 589856 | tf_op jit(solution)/shard_map/ppermute | solution.py:22
  451.6 3.7 unpack.6
  455.4 8.1 %collective-permute-done.65.far = bf16[2,2,192,384]{3,2,1,0:T(8,128)(2,1)S(1)} collective-permute-done((bf16[2,2,192,384]{3,2,1,0:T(8,128)(2,1)S(1)}, bf16[2,2,192,384]{3,2,1,0:T(8,128)(2,1)S(1)}, u32[]{:S(2)}, u32[]{:S(2)}) %collective-permute-start.65) | collective-permute-done | bytes 589856 | tf_op jit(solution)/shard_map/ppermute | solution.py:22
  464.2 3.7 unpack.11
  468.8 3.7 unpack.9
  472.5 1.8 collective-permute-done.61.far
  475.2 3.8 unpack.7
  (232 shorter events, 77.6 us)
Async XLA Ops:
  0.6 20.9 %collective-permute-start.1 = (bf16[2,192,2304]{2,1,0:T(8,128)(2,1)}, bf16[2,192,2304]{2,1,0:T(8,128)(2,1)}, u32[]{:S(2)}, u32[]{:S(2)}) collective-permute-start(bf16[2,192,2304]{2,1,0:T(8,128)(2,1)} %rest_0_.15), channel_id=1, source_target_pairs={{0,1},{1,0},{2,3},{3,2},{4,5},{5,4},{6,7},{7,6},{8,9},{9,8},{10,11... | collective-permute-start | bytes 5308424 | tf_op jit(solution)/shard_map/ppermute | solution.py:22
  1.2 11.9 %collective-permute-start.2 = (bf16[2,192,768]{2,1,0:T(8,128)(2,1)}, bf16[2,192,768]{2,1,0:T(8,128)(2,1)}, u32[]{:S(2)}, u32[]{:S(2)}) collective-permute-start(bf16[2,192,768]{2,1,0:T(8,128)(2,1)} %rest_2_.7), channel_id=1, source_target_pairs={{0,1},{1,0},{2,3},{3,2},{4,5},{5,4},{6,7},{7,6},{8,9},{9,8},{10,11... | collective-permute-start | bytes 1769480 | tf_op jit(solution)/shard_map/ppermute | solution.py:22
  4.3 17.2 %collective-permute-start = (bf16[96,3072]{1,0:T(8,128)(2,1)}, bf16[96,3072]{1,0:T(8,128)(2,1)S(1)}, u32[]{:S(2)}, u32[]{:S(2)}) collective-permute-start(bf16[96,3072]{1,0:T(8,128)(2,1)} %pad_maximum_fusion.1), channel_id=1, source_target_pairs={{0,2},{1,3},{2,0},{3,1},{4,6},{5,7},{6,4},{7,5},{8,10},{9,11},{10,... | collective-permute-start | bytes 1769480 | tf_op jit(solution)/shard_map/ppermute | solution.py:22
  13.0 22.0 %collective-permute-start.4 = (bf16[96,3072]{1,0:T(8,128)(2,1)S(1)}, bf16[96,3072]{1,0:T(8,128)(2,1)S(1)}, u32[]{:S(2)}, u32[]{:S(2)}) collective-permute-start(bf16[96,3072]{1,0:T(8,128)(2,1)S(1)} %get-tuple-element.193), channel_id=1, source_target_pairs={{0,2},{1,3},{2,0},{3,1},{4,6},{5,7},{6,4},{7,5},{8,10},{9,11},{10,... | collective-permute-start | bytes 1769480 | tf_op jit(solution)/shard_map/ppermute | solution.py:22
  21.6 14.2 %collective-permute-start.3 = (bf16[96,3072]{1,0:T(8,128)(2,1)S(1)}, bf16[96,3072]{1,0:T(8,128)(2,1)S(1)}, u32[]{:S(2)}, u32[]{:S(2)}) collective-permute-start(bf16[96,3072]{1,0:T(8,128)(2,1)S(1)} %collective-permute-done.rest_4_), channel_id=1, source_target_pairs={{0,4},{4,0},{8,12},{12,8},{16,20},{20,16},{24,28},{28,24},{1,5},{5... | collective-permute-start | bytes 1769480 | tf_op jit(solution)/shard_map/ppermute | solution.py:22
  23.7 10.3 %collective-permute-start.7 = (f32[2,12,192]{2,1,0:T(8,128)S(1)}, f32[2,12,192]{2,1,0:T(8,128)S(1)}, u32[]{:S(2)}, u32[]{:S(2)}) collective-permute-start(f32[2,12,192]{2,1,0:T(8,128)S(1)} %copy-done.33), channel_id=1, source_target_pairs={{0,3},{1,2},{2,1},{3,0},{4,7},{5,6},{6,5},{7,4},{8,11},{9,10},{10,... | collective-permute-start | bytes 55304 | tf_op jit(solution)/shard_map/ppermute | solution.py:595
  23.7 11.4 %collective-permute-start.6 = (f32[2,12,192]{2,1,0:T(8,128)S(1)}, f32[2,12,192]{2,1,0:T(8,128)S(1)}, u32[]{:S(2)}, u32[]{:S(2)}) collective-permute-start(f32[2,12,192]{2,1,0:T(8,128)S(1)} %copy-done.33), channel_id=1, source_target_pairs={{0,2},{1,3},{2,0},{3,1},{4,6},{5,7},{6,4},{7,5},{8,10},{9,11},{10,... | collective-permute-start | bytes 55304 | tf_op jit(solution)/shard_map/ppermute | solution.py:595
  25.2 9.9 %collective-permute-start.5 = (f32[2,12,192]{2,1,0:T(8,128)S(1)}, f32[2,12,192]{2,1,0:T(8,128)S(1)}, u32[]{:S(2)}, u32[]{:S(2)}) collective-permute-start(f32[2,12,192]{2,1,0:T(8,128)S(1)} %copy-done.33), channel_id=1, source_target_pairs={{0,1},{1,0},{2,3},{3,2},{4,5},{5,4},{6,7},{7,6},{8,9},{9,8},{10,11... | collective-permute-start | bytes 55304 | tf_op jit(solution)/shard_map/ppermute | solution.py:595
  34.0 13.7 %collective-permute-start.11 = (bf16[2,768,768]{2,1,0:T(8,128)(2,1)}, bf16[2,768,768]{2,1,0:T(8,128)(2,1)}, u32[]{:S(2)}, u32[]{:S(2)}) collective-permute-start(bf16[2,768,768]{2,1,0:T(8,128)(2,1)} %rest_5_.7), channel_id=1, source_target_pairs={{0,1},{1,0},{2,3},{3,2},{4,5},{5,4},{6,7},{7,6},{8,9},{9,8},{10,11... | collective-permute-start | bytes 7077896 | tf_op jit(solution)/shard_map/ppermute | solution.py:22
  36.7 10.9 %collective-permute-start.10 = (bf16[2,192,3072]{2,1,0:T(8,128)(2,1)S(1)}, bf16[2,192,3072]{2,1,0:T(8,128)(2,1)}, u32[]{:S(2)}, u32[]{:S(2)}) collective-permute-start(bf16[2,192,3072]{2,1,0:T(8,128)(2,1)S(1)} %copy-done), channel_id=1, source_target_pairs={{0,1},{1,0},{2,3},{3,2},{4,5},{5,4},{6,7},{7,6},{8,9},{9,8},{10,11... | collective-permute-start | bytes 7077896 | tf_op jit(solution)/shard_map/ppermute | solution.py:22
  36.9 10.8 %collective-permute-start.12 = (bf16[192,3072]{1,0:T(8,128)(2,1)}, bf16[192,3072]{1,0:T(8,128)(2,1)}, u32[]{:S(2)}, u32[]{:S(2)}) collective-permute-start(bf16[192,3072]{1,0:T(8,128)(2,1)} %constant_dynamic-update-slice_fusion), channel_id=1, source_target_pairs={{0,1},{1,0},{2,3},{3,2},{4,5},{5,4},{6,7},{7,6},{8,9},{9,8},{10,11... | collective-permute-start | bytes 3538952 | tf_op jit(solution)/shard_map/ppermute | solution.py:22
  38.0 16.8 %collective-permute-start.8 = (bf16[96,3072]{1,0:T(8,128)(2,1)S(1)}, bf16[96,3072]{1,0:T(8,128)(2,1)S(1)}, u32[]{:S(2)}, u32[]{:S(2)}) collective-permute-start(bf16[96,3072]{1,0:T(8,128)(2,1)S(1)} %collective-permute-done.4.rest_2_), channel_id=1, source_target_pairs={{0,4},{4,0},{8,12},{12,8},{16,20},{20,16},{24,28},{28,24},{1,5},{5... | collective-permute-start | bytes 1769480 | tf_op jit(solution)/shard_map/ppermute | solution.py:22
  39.4 15.3 %collective-permute-start.9 = (bf16[384,768]{1,0:T(8,128)(2,1)}, bf16[384,768]{1,0:T(8,128)(2,1)}, u32[]{:S(2)}, u32[]{:S(2)}) collective-permute-start(bf16[384,768]{1,0:T(8,128)(2,1)} %get-tuple-element.209), channel_id=1, source_target_pairs={{0,2},{1,3},{2,0},{3,1},{4,6},{5,7},{6,4},{7,5},{8,10},{9,11},{10,... | collective-permute-start | bytes 1769480 | tf_op jit(solution)/shard_map/ppermute | solution.py:22
  54.8 12.0 %collective-permute-start.15 = (bf16[192,3072]{1,0:T(8,128)(2,1)S(1)}, bf16[192,3072]{1,0:T(8,128)(2,1)S(1)}, u32[]{:S(2)}, u32[]{:S(2)}) collective-permute-start(bf16[192,3072]{1,0:T(8,128)(2,1)S(1)} %constant_dynamic-update-slice_fusion.2), channel_id=1, source_target_pairs={{0,1},{1,0},{2,3},{3,2},{4,5},{5,4},{6,7},{7,6},{8,9},{9,8},{10,11... | collective-permute-start | bytes 3538952 | tf_op jit(solution)/shard_map/ppermute | solution.py:22
  54.9 15.7 %collective-permute-start.14 = (bf16[96,3072]{1,0:T(8,128)(2,1)S(1)}, bf16[96,3072]{1,0:T(8,128)(2,1)S(1)}, u32[]{:S(2)}, u32[]{:S(2)}) collective-permute-start(bf16[96,3072]{1,0:T(8,128)(2,1)S(1)} %copy-done.28), channel_id=1, source_target_pairs={{0,2},{1,3},{2,0},{3,1},{4,6},{5,7},{6,4},{7,5},{8,10},{9,11},{10,... | collective-permute-start | bytes 1769480 | tf_op jit(solution)/shard_map/ppermute | solution.py:22
  56.4 15.6 %collective-permute-start.13 = (bf16[384,768]{1,0:T(8,128)(2,1)}, bf16[384,768]{1,0:T(8,128)(2,1)S(1)}, u32[]{:S(2)}, u32[]{:S(2)}) collective-permute-start(bf16[384,768]{1,0:T(8,128)(2,1)} %collective-permute-done.9.rest_7_), channel_id=1, source_target_pairs={{0,4},{4,0},{8,12},{12,8},{16,20},{20,16},{24,28},{28,24},{1,5},{5... | collective-permute-start | bytes 1769480 | tf_op jit(solution)/shard_map/ppermute | solution.py:22
  72.2 15.7 %collective-permute-start.18 = (bf16[96,3072]{1,0:T(8,128)(2,1)S(1)}, bf16[96,3072]{1,0:T(8,128)(2,1)S(1)}, u32[]{:S(2)}, u32[]{:S(2)}) collective-permute-start(bf16[96,3072]{1,0:T(8,128)(2,1)S(1)} %copy-done.24), channel_id=1, source_target_pairs={{0,2},{1,3},{2,0},{3,1},{4,6},{5,7},{6,4},{7,5},{8,10},{9,11},{10,... | collective-permute-start | bytes 1769480 | tf_op jit(solution)/shard_map/ppermute | solution.py:22
  72.8 15.4 %collective-permute-start.17 = (bf16[96,3072]{1,0:T(8,128)(2,1)S(1)}, bf16[96,3072]{1,0:T(8,128)(2,1)S(1)}, u32[]{:S(2)}, u32[]{:S(2)}) collective-permute-start(bf16[96,3072]{1,0:T(8,128)(2,1)S(1)} %collective-permute-done.14.rest_4_), channel_id=1, source_target_pairs={{0,4},{4,0},{8,12},{12,8},{16,20},{20,16},{24,28},{28,24},{1,5},{5... | collective-permute-start | bytes 1769480 | tf_op jit(solution)/shard_map/ppermute | solution.py:22
  88.2 2.9 collective-permute-start.19
  88.3 16.5 %collective-permute-start.20 = (bf16[96,3072]{1,0:T(8,128)(2,1)S(1)}, bf16[96,3072]{1,0:T(8,128)(2,1)S(1)}, u32[]{:S(2)}, u32[]{:S(2)}) collective-permute-start(bf16[96,3072]{1,0:T(8,128)(2,1)S(1)} %collective-permute-done.18.rest_2_), channel_id=1, source_target_pairs={{0,4},{4,0},{8,12},{12,8},{16,20},{20,16},{24,28},{28,24},{1,5},{5... | collective-permute-start | bytes 1769480 | tf_op jit(solution)/shard_map/ppermute | solution.py:22
  89.4 15.4 %collective-permute-start.21 = (bf16[384,768]{1,0:T(8,128)(2,1)S(1)}, bf16[384,768]{1,0:T(8,128)(2,1)S(1)}, u32[]{:S(2)}, u32[]{:S(2)}) collective-permute-start(bf16[384,768]{1,0:T(8,128)(2,1)S(1)} %copy-done.23), channel_id=1, source_target_pairs={{0,2},{1,3},{2,0},{3,1},{4,6},{5,7},{6,4},{7,5},{8,10},{9,11},{10,... | collective-permute-start | bytes 1769480 | tf_op jit(solution)/shard_map/ppermute | solution.py:22
  104.9 15.7 %collective-permute-start.22 = (bf16[384,768]{1,0:T(8,128)(2,1)S(1)}, bf16[384,768]{1,0:T(8,128)(2,1)S(1)}, u32[]{:S(2)}, u32[]{:S(2)}) collective-permute-start(bf16[384,768]{1,0:T(8,128)(2,1)S(1)} %collective-permute-done.21.rest_7_), channel_id=1, source_target_pairs={{0,4},{4,0},{8,12},{12,8},{16,20},{20,16},{24,28},{28,24},{1,5},{5... | collective-permute-start | bytes 1769480 | tf_op jit(solution)/shard_map/ppermute | solution.py:22
  141.4 15.4 %collective-permute-start.26 = (bf16[2,2,2,2,192,384]{5,4,3,2,1,0:T(8,128)(2,1)}, bf16[2,2,2,2,192,384]{5,4,3,2,1,0:T(8,128)(2,1)S(1)}, u32[]{:S(2)}, u32[]{:S(2)}) collective-permute-start(bf16[2,2,2,2,192,384]{5,4,3,2,1,0:T(8,128)(2,1)} %get-tuple-element.257), channel_id=1, source_target_pairs={{0,1},{1,0},{2,3},{3,2},{4,5},{5,4},{6,7},{7,6},{8,9},{9,8},{10,11... | collective-permute-start | bytes 7077896 | tf_op jit(solution)/shard_map/ppermute | solution.py:22
  156.3 4.9 %collective-permute-start.25 = (bf16[2,2,2,2,192,384]{5,4,3,2,1,0:T(8,128)(2,1)}, bf16[2,2,2,2,192,384]{5,4,3,2,1,0:T(8,128)(2,1)S(1)}, u32[]{:S(2)}, u32[]{:S(2)}) collective-permute-start(bf16[2,2,2,2,192,384]{5,4,3,2,1,0:T(8,128)(2,1)} %get-tuple-element.255), channel_id=1, source_target_pairs={{0,1},{1,0},{2,3},{3,2},{4,5},{5,4},{6,7},{7,6},{8,9},{9,8},{10,11... | collective-permute-start | bytes 7077896 | tf_op jit(solution)/shard_map/ppermute | solution.py:22
  174.9 36.8 %collective-permute-start.31 = (bf16[2,2,2,2,192,384]{5,4,3,2,1,0:T(8,128)(2,1)}, bf16[2,2,2,2,192,384]{5,4,3,2,1,0:T(8,128)(2,1)S(1)}, u32[]{:S(2)}, u32[]{:S(2)}) collective-permute-start(bf16[2,2,2,2,192,384]{5,4,3,2,1,0:T(8,128)(2,1)} %get-tuple-element.276), channel_id=1, source_target_pairs={{0,1},{1,0},{2,3},{3,2},{4,5},{5,4},{6,7},{7,6},{8,9},{9,8},{10,11... | collective-permute-start | bytes 7077896 | tf_op jit(solution)/shard_map/ppermute | solution.py:22
  181.4 32.7 %collective-permute-start.29 = (bf16[2,2,2,2,192,384]{5,4,3,2,1,0:T(8,128)(2,1)}, bf16[2,2,2,2,192,384]{5,4,3,2,1,0:T(8,128)(2,1)S(1)}, u32[]{:S(2)}, u32[]{:S(2)}) collective-permute-start(bf16[2,2,2,2,192,384]{5,4,3,2,1,0:T(8,128)(2,1)} %get-tuple-element.274), channel_id=1, source_target_pairs={{0,1},{1,0},{2,3},{3,2},{4,5},{5,4},{6,7},{7,6},{8,9},{9,8},{10,11... | collective-permute-start | bytes 7077896 | tf_op jit(solution)/shard_map/ppermute | solution.py:22
  181.6 28.3 %collective-permute-start.27 = (bf16[2,2,2,192,384]{4,3,2,1,0:T(8,128)(2,1)S(1)}, bf16[2,2,2,192,384]{4,3,2,1,0:T(8,128)(2,1)S(1)}, u32[]{:S(2)}, u32[]{:S(2)}) collective-permute-start(bf16[2,2,2,192,384]{4,3,2,1,0:T(8,128)(2,1)S(1)} %get-tuple-element.366), channel_id=1, source_target_pairs={{0,2},{1,3},{2,0},{3,1},{4,6},{5,7},{6,4},{7,5},{8,10},{9,11},{10,... | collective-permute-start | bytes 3538952 | tf_op jit(solution)/shard_map/ppermute | solution.py:22
  182.9 29.5 %collective-permute-start.30 = (bf16[2,2,2,192,384]{4,3,2,1,0:T(8,128)(2,1)S(1)}, bf16[2,2,2,192,384]{4,3,2,1,0:T(8,128)(2,1)S(1)}, u32[]{:S(2)}, u32[]{:S(2)}) collective-permute-start(bf16[2,2,2,192,384]{4,3,2,1,0:T(8,128)(2,1)S(1)} %get-tuple-element.364), channel_id=1, source_target_pairs={{0,8},{4,12},{8,0},{12,4},{16,24},{20,28},{24,16},{28,20},{1,9},{5... | collective-permute-start | bytes 3538952 | tf_op jit(solution)/shard_map/ppermute | solution.py:22
  210.2 14.9 %collective-permute-start.28 = (bf16[2,2,192,384]{3,2,1,0:T(8,128)(2,1)S(1)}, bf16[2,2,192,384]{3,2,1,0:T(8,128)(2,1)S(1)}, u32[]{:S(2)}, u32[]{:S(2)}) collective-permute-start(bf16[2,2,192,384]{3,2,1,0:T(8,128)(2,1)S(1)} %get-tuple-element.377), channel_id=1, source_target_pairs={{0,4},{4,0},{8,12},{12,8},{16,20},{20,16},{24,28},{28,24},{1,5},{5... | collective-permute-start | bytes 1769480 | tf_op jit(solution)/shard_map/ppermute | solution.py:22
  212.7 14.8 %collective-permute-start.33 = (bf16[2,2,192,384]{3,2,1,0:T(8,128)(2,1)S(1)}, bf16[2,2,192,384]{3,2,1,0:T(8,128)(2,1)S(1)}, u32[]{:S(2)}, u32[]{:S(2)}) collective-permute-start(bf16[2,2,192,384]{3,2,1,0:T(8,128)(2,1)S(1)} %get-tuple-element.376), channel_id=1, source_target_pairs={{0,2},{1,3},{2,0},{3,1},{4,6},{5,7},{6,4},{7,5},{8,10},{9,11},{10,... | collective-permute-start | bytes 1769480 | tf_op jit(solution)/shard_map/ppermute | solution.py:22
  225.2 7.7 %collective-permute-start.32 = (bf16[2,192,384]{2,1,0:T(8,128)(2,1)S(1)}, bf16[2,192,384]{2,1,0:T(8,128)(2,1)S(1)}, u32[]{:S(2)}, u32[]{:S(2)}) collective-permute-start(bf16[2,192,384]{2,1,0:T(8,128)(2,1)S(1)} %fusion.45), channel_id=1, source_target_pairs={{0,8},{4,12},{8,0},{12,4},{16,24},{20,28},{24,16},{28,20},{1,9},{5... | collective-permute-start | bytes 884744 | tf_op jit(solution)/shard_map/ppermute | solution.py:22
  247.9 30.9 %collective-permute-start.39 = (bf16[2,2,2,2,192,384]{5,4,3,2,1,0:T(8,128)(2,1)}, bf16[2,2,2,2,192,384]{5,4,3,2,1,0:T(8,128)(2,1)S(1)}, u32[]{:S(2)}, u32[]{:S(2)}) collective-permute-start(bf16[2,2,2,2,192,384]{5,4,3,2,1,0:T(8,128)(2,1)} %get-tuple-element.291), channel_id=1, source_target_pairs={{0,1},{1,0},{2,3},{3,2},{4,5},{5,4},{6,7},{7,6},{8,9},{9,8},{10,11... | collective-permute-start | bytes 7077896 | tf_op jit(solution)/shard_map/ppermute | solution.py:22
  248.0 28.8 %collective-permute-start.36 = (bf16[2,2,2,192,384]{4,3,2,1,0:T(8,128)(2,1)S(1)}, bf16[2,2,2,192,384]{4,3,2,1,0:T(8,128)(2,1)S(1)}, u32[]{:S(2)}, u32[]{:S(2)}) collective-permute-start(bf16[2,2,2,192,384]{4,3,2,1,0:T(8,128)(2,1)S(1)} %get-tuple-element.360), channel_id=1, source_target_pairs={{0,4},{4,0},{8,12},{12,8},{16,20},{20,16},{24,28},{28,24},{1,5},{5... | collective-permute-start | bytes 3538952 | tf_op jit(solution)/shard_map/ppermute | solution.py:22
  249.5 27.6 %collective-permute-start.35 = (bf16[2,192,384]{2,1,0:T(8,128)(2,1)S(1)}, bf16[2,192,384]{2,1,0:T(8,128)(2,1)S(1)}, u32[]{:S(2)}, u32[]{:S(2)}) collective-permute-start(bf16[2,192,384]{2,1,0:T(8,128)(2,1)S(1)} %fusion.40), channel_id=1, source_target_pairs={{0,16},{4,20},{8,24},{12,28},{16,0},{20,4},{24,8},{28,12},{1,17},{... | collective-permute-start | bytes 884744 | tf_op jit(solution)/shard_map/ppermute | solution.py:22
  252.1 33.4 %collective-permute-start.34 = (bf16[2,2,2,192,384]{4,3,2,1,0:T(8,128)(2,1)S(1)}, bf16[2,2,2,192,384]{4,3,2,1,0:T(8,128)(2,1)S(1)}, u32[]{:S(2)}, u32[]{:S(2)}) collective-permute-start(bf16[2,2,2,192,384]{4,3,2,1,0:T(8,128)(2,1)S(1)} %get-tuple-element.362), channel_id=1, source_target_pairs={{0,2},{1,3},{2,0},{3,1},{4,6},{5,7},{6,4},{7,5},{8,10},{9,11},{10,... | collective-permute-start | bytes 3538952 | tf_op jit(solution)/shard_map/ppermute | solution.py:22
  253.2 29.5 %collective-permute-start.38 = (bf16[2,192,384]{2,1,0:T(8,128)(2,1)S(1)}, bf16[2,192,384]{2,1,0:T(8,128)(2,1)S(1)}, u32[]{:S(2)}, u32[]{:S(2)}) collective-permute-start(bf16[2,192,384]{2,1,0:T(8,128)(2,1)S(1)} %fusion.46), channel_id=1, source_target_pairs={{0,4},{4,0},{8,12},{12,8},{16,20},{20,16},{24,28},{28,24},{1,5},{5... | collective-permute-start | bytes 884744 | tf_op jit(solution)/shard_map/ppermute | solution.py:22
  277.2 8.2 %collective-permute-start.37 = (bf16[1,2,192,384]{3,2,1,0:T(8,128)(2,1)S(1)}, bf16[1,2,192,384]{3,2,1,0:T(8,128)(2,1)S(1)}, u32[]{:S(2)}, u32[]{:S(2)}) collective-permute-start(bf16[1,2,192,384]{3,2,1,0:T(8,128)(2,1)S(1)} %bitcast.236), channel_id=1, source_target_pairs={{0,8},{4,12},{8,0},{12,4},{16,24},{20,28},{24,16},{28,20},{1,9},{5... | collective-permute-start | bytes 884744 | tf_op jit(solution)/shard_map/ppermute | solution.py:22
  298.7 20.8 %collective-permute-start.40 = (bf16[2,2,2,2,208,384]{5,4,3,2,1,0:T(8,128)(2,1)}, bf16[2,2,2,2,208,384]{5,4,3,2,1,0:T(8,128)(2,1)S(1)}, u32[]{:S(2)}, u32[]{:S(2)}) collective-permute-start(bf16[2,2,2,2,208,384]{5,4,3,2,1,0:T(8,128)(2,1)} %get-tuple-element.304), channel_id=1, source_target_pairs={{0,1},{1,0},{2,3},{3,2},{4,5},{5,4},{6,7},{7,6},{8,9},{9,8},{10,11... | collective-permute-start | bytes 7667720 | tf_op jit(solution)/shard_map/ppermute | solution.py:22
  298.8 15.7 %collective-permute-start.42 = (bf16[2,2,192,384]{3,2,1,0:T(8,128)(2,1)S(1)}, bf16[2,2,192,384]{3,2,1,0:T(8,128)(2,1)S(1)}, u32[]{:S(2)}, u32[]{:S(2)}) collective-permute-start(bf16[2,2,192,384]{3,2,1,0:T(8,128)(2,1)S(1)} %get-tuple-element.374), channel_id=1, source_target_pairs={{0,2},{1,3},{2,0},{3,1},{4,6},{5,7},{6,4},{7,5},{8,10},{9,11},{10,... | collective-permute-start | bytes 1769480 | tf_op jit(solution)/shard_map/ppermute | solution.py:22
  299.9 17.9 %collective-permute-start.41 = (bf16[2,192,384]{2,1,0:T(8,128)(2,1)S(1)}, bf16[2,192,384]{2,1,0:T(8,128)(2,1)S(1)}, u32[]{:S(2)}, u32[]{:S(2)}) collective-permute-start(bf16[2,192,384]{2,1,0:T(8,128)(2,1)S(1)} %fusion.36), channel_id=1, source_target_pairs={{0,16},{4,20},{8,24},{12,28},{16,0},{20,4},{24,8},{28,12},{1,17},{... | collective-permute-start | bytes 884744 | tf_op jit(solution)/shard_map/ppermute | solution.py:22
  314.5 16.2 %collective-permute-start.45 = (bf16[2,2,192,384]{3,2,1,0:T(8,128)(2,1)S(1)}, bf16[2,2,192,384]{3,2,1,0:T(8,128)(2,1)S(1)}, u32[]{:S(2)}, u32[]{:S(2)}) collective-permute-start(bf16[2,2,192,384]{3,2,1,0:T(8,128)(2,1)S(1)} %get-tuple-element.372), channel_id=1, source_target_pairs={{0,8},{4,12},{8,0},{12,4},{16,24},{20,28},{24,16},{28,20},{1,9},{5... | collective-permute-start | bytes 1769480 | tf_op jit(solution)/shard_map/ppermute | solution.py:22
  316.0 28.9 %collective-permute-start.47 = (bf16[2,2,2,192,384]{4,3,2,1,0:T(8,128)(2,1)S(1)}, bf16[2,2,2,192,384]{4,3,2,1,0:T(8,128)(2,1)S(1)}, u32[]{:S(2)}, u32[]{:S(2)}) collective-permute-start(bf16[2,2,2,192,384]{4,3,2,1,0:T(8,128)(2,1)S(1)} %get-tuple-element.358), channel_id=1, source_target_pairs={{0,2},{1,3},{2,0},{3,1},{4,6},{5,7},{6,4},{7,5},{8,10},{9,11},{10,... | collective-permute-start | bytes 3538952 | tf_op jit(solution)/shard_map/ppermute | solution.py:22
  317.2 19.9 %collective-permute-start.44 = (bf16[2,192,384]{2,1,0:T(8,128)(2,1)S(1)}, bf16[2,192,384]{2,1,0:T(8,128)(2,1)S(1)}, u32[]{:S(2)}, u32[]{:S(2)}) collective-permute-start(bf16[2,192,384]{2,1,0:T(8,128)(2,1)S(1)} %fusion.48), channel_id=1, source_target_pairs={{0,8},{4,12},{8,0},{12,4},{16,24},{20,28},{24,16},{28,20},{1,9},{5... | collective-permute-start | bytes 884744 | tf_op jit(solution)/shard_map/ppermute | solution.py:22
  317.8 32.1 %collective-permute-start.50 = (bf16[1,2,192,384]{3,2,1,0:T(8,128)(2,1)S(1)}, bf16[1,2,192,384]{3,2,1,0:T(8,128)(2,1)S(1)}, u32[]{:S(2)}, u32[]{:S(2)}) collective-permute-start(bf16[1,2,192,384]{3,2,1,0:T(8,128)(2,1)S(1)} %bitcast.230), channel_id=1, source_target_pairs={{0,8},{4,12},{8,0},{12,4},{16,24},{20,28},{24,16},{28,20},{1,9},{5... | collective-permute-start | bytes 884744 | tf_op jit(solution)/shard_map/ppermute | solution.py:22
  321.8 48.9 %collective-permute-start.43 = (bf16[2,2,2,208,384]{4,3,2,1,0:T(8,128)(2,1)S(1)}, bf16[2,2,2,208,384]{4,3,2,1,0:T(8,128)(2,1)S(1)}, u32[]{:S(2)}, u32[]{:S(2)}) collective-permute-start(bf16[2,2,2,208,384]{4,3,2,1,0:T(8,128)(2,1)S(1)} %get-tuple-element.355), channel_id=1, source_target_pairs={{0,2},{1,3},{2,0},{3,1},{4,6},{5,7},{6,4},{7,5},{8,10},{9,11},{10,... | collective-permute-start | bytes 3833864 | tf_op jit(solution)/shard_map/ppermute | solution.py:22
  345.2 18.5 %collective-permute-start.48 = (bf16[2,2,192,384]{3,2,1,0:T(8,128)(2,1)S(1)}, bf16[2,2,192,384]{3,2,1,0:T(8,128)(2,1)S(1)}, u32[]{:S(2)}, u32[]{:S(2)}) collective-permute-start(bf16[2,2,192,384]{3,2,1,0:T(8,128)(2,1)S(1)} %get-tuple-element.369), channel_id=1, source_target_pairs={{0,4},{4,0},{8,12},{12,8},{16,20},{20,16},{24,28},{28,24},{1,5},{5... | collective-permute-start | bytes 1769480 | tf_op jit(solution)/shard_map/ppermute | solution.py:22
  346.8 16.9 %collective-permute-start.49 = (bf16[2,192,384]{2,1,0:T(8,128)(2,1)S(1)}, bf16[2,192,384]{2,1,0:T(8,128)(2,1)S(1)}, u32[]{:S(2)}, u32[]{:S(2)}) collective-permute-start(bf16[2,192,384]{2,1,0:T(8,128)(2,1)S(1)} %fusion.50), channel_id=1, source_target_pairs={{0,4},{4,0},{8,12},{12,8},{16,20},{20,16},{24,28},{28,24},{1,5},{5... | collective-permute-start | bytes 884744 | tf_op jit(solution)/shard_map/ppermute | solution.py:22
  347.3 16.5 %collective-permute-start.46 = (bf16[2,192,384]{2,1,0:T(8,128)(2,1)S(1)}, bf16[2,192,384]{2,1,0:T(8,128)(2,1)S(1)}, u32[]{:S(2)}, u32[]{:S(2)}) collective-permute-start(bf16[2,192,384]{2,1,0:T(8,128)(2,1)S(1)} %fusion.33), channel_id=1, source_target_pairs={{0,16},{4,20},{8,24},{12,28},{16,0},{20,4},{24,8},{28,12},{1,17},{... | collective-permute-start | bytes 884744 | tf_op jit(solution)/shard_map/ppermute | solution.py:22
  364.1 13.7 %collective-permute-start.52 = (bf16[1,2,192,384]{3,2,1,0:T(8,128)(2,1)S(1)}, bf16[1,2,192,384]{3,2,1,0:T(8,128)(2,1)S(1)}, u32[]{:S(2)}, u32[]{:S(2)}) collective-permute-start(bf16[1,2,192,384]{3,2,1,0:T(8,128)(2,1)S(1)} %bitcast.232), channel_id=1, source_target_pairs={{0,8},{4,12},{8,0},{12,4},{16,24},{20,28},{24,16},{28,20},{1,9},{5... | collective-permute-start | bytes 884744 | tf_op jit(solution)/shard_map/ppermute | solution.py:22
  364.7 16.9 %collective-permute-start.54 = (bf16[2,192,384]{2,1,0:T(8,128)(2,1)S(1)}, bf16[2,192,384]{2,1,0:T(8,128)(2,1)S(1)}, u32[]{:S(2)}, u32[]{:S(2)}) collective-permute-start(bf16[2,192,384]{2,1,0:T(8,128)(2,1)S(1)} %fusion.51), channel_id=1, source_target_pairs={{0,8},{4,12},{8,0},{12,4},{16,24},{20,28},{24,16},{28,20},{1,9},{5... | collective-permute-start | bytes 884744 | tf_op jit(solution)/shard_map/ppermute | solution.py:22
  366.2 15.5 %collective-permute-start.56 = (bf16[2,192,384]{2,1,0:T(8,128)(2,1)S(1)}, bf16[2,192,384]{2,1,0:T(8,128)(2,1)S(1)}, u32[]{:S(2)}, u32[]{:S(2)}) collective-permute-start(bf16[2,192,384]{2,1,0:T(8,128)(2,1)S(1)} %fusion.29), channel_id=1, source_target_pairs={{0,16},{4,20},{8,24},{12,28},{16,0},{20,4},{24,8},{28,12},{1,17},{... | collective-permute-start | bytes 884744 | tf_op jit(solution)/shard_map/ppermute | solution.py:22
  371.0 14.8 %collective-permute-start.51 = (bf16[2,2,208,384]{3,2,1,0:T(8,128)(2,1)S(1)}, bf16[2,2,208,384]{3,2,1,0:T(8,128)(2,1)S(1)}, u32[]{:S(2)}, u32[]{:S(2)}) collective-permute-start(bf16[2,2,208,384]{3,2,1,0:T(8,128)(2,1)S(1)} %get-tuple-element.367), channel_id=1, source_target_pairs={{0,4},{4,0},{8,12},{12,8},{16,20},{20,16},{24,28},{28,24},{1,5},{5... | collective-permute-start | bytes 1916936 | tf_op jit(solution)/shard_map/ppermute | solution.py:22
  381.9 14.3 %collective-permute-start.57 = (bf16[1,2,192,384]{3,2,1,0:T(8,128)(2,1)S(1)}, bf16[1,2,192,384]{3,2,1,0:T(8,128)(2,1)S(1)}, u32[]{:S(2)}, u32[]{:S(2)}) collective-permute-start(bf16[1,2,192,384]{3,2,1,0:T(8,128)(2,1)S(1)} %bitcast.238), channel_id=1, source_target_pairs={{0,8},{4,12},{8,0},{12,4},{16,24},{20,28},{24,16},{28,20},{1,9},{5... | collective-permute-start | bytes 884744 | tf_op jit(solution)/shard_map/ppermute | solution.py:22
  385.3 11.9 %collective-permute-start.55 = (bf16[2,192,384]{2,1,0:T(8,128)(2,1)S(1)}, bf16[2,192,384]{2,1,0:T(8,128)(2,1)S(1)}, u32[]{:S(2)}, u32[]{:S(2)}) collective-permute-start(bf16[2,192,384]{2,1,0:T(8,128)(2,1)S(1)} %fusion.27), channel_id=1, source_target_pairs={{0,16},{4,20},{8,24},{12,28},{16,0},{20,4},{24,8},{28,12},{1,17},{... | collective-permute-start | bytes 884744 | tf_op jit(solution)/shard_map/ppermute | solution.py:22
  385.9 15.7 %collective-permute-start.53 = (bf16[2,208,384]{2,1,0:T(8,128)(2,1)S(1)}, bf16[2,208,384]{2,1,0:T(8,128)(2,1)S(1)}, u32[]{:S(2)}, u32[]{:S(2)}) collective-permute-start(bf16[2,208,384]{2,1,0:T(8,128)(2,1)S(1)} %fusion.43), channel_id=1, source_target_pairs={{0,8},{4,12},{8,0},{12,4},{16,24},{20,28},{24,16},{28,20},{1,9},{5... | collective-permute-start | bytes 958472 | tf_op jit(solution)/shard_map/ppermute | solution.py:22
  401.7 15.4 %collective-permute-start.58 = (bf16[2,208,384]{2,1,0:T(8,128)(2,1)S(1)}, bf16[2,208,384]{2,1,0:T(8,128)(2,1)S(1)}, u32[]{:S(2)}, u32[]{:S(2)}) collective-permute-start(bf16[2,208,384]{2,1,0:T(8,128)(2,1)S(1)} %fusion.20), channel_id=1, source_target_pairs={{0,16},{4,20},{8,24},{12,28},{16,0},{20,4},{24,8},{28,12},{1,17},{... | collective-permute-start | bytes 958472 | tf_op jit(solution)/shard_map/ppermute | solution.py:22
  404.0 25.1 %collective-permute-start.66 = (bf16[2,2,192,384]{3,2,1,0:T(8,128)(2,1)S(1)}, bf16[2,2,192,384]{3,2,1,0:T(8,128)(2,1)S(1)}, u32[]{:S(2)}, u32[]{:S(2)}) collective-permute-start(bf16[2,2,192,384]{3,2,1,0:T(8,128)(2,1)S(1)} %pad_maximum_fusion.3.near), channel_id=1, source_target_pairs={{0,4},{4,0},{8,12},{12,8},{16,20},{20,16},{24,28},{28,24},{1,5},{5... | collective-permute-start | bytes 1769480 | tf_op jit(solution)/shard_map/ppermute | solution.py:22
  405.5 20.1 %collective-permute-start.60 = (bf16[1,2,192,384]{3,2,1,0:T(8,128)(2,1)S(1)}, bf16[1,2,192,384]{3,2,1,0:T(8,128)(2,1)S(1)}, u32[]{:S(2)}, u32[]{:S(2)}) collective-permute-start(bf16[1,2,192,384]{3,2,1,0:T(8,128)(2,1)S(1)} %bitcast.234), channel_id=1, source_target_pairs={{0,4},{4,0},{8,12},{12,8},{16,20},{20,16},{24,28},{28,24},{1,5},{5... | collective-permute-start | bytes 884744 | tf_op jit(solution)/shard_map/ppermute | solution.py:22
  417.2 10.0 %collective-permute-start.59 = (bf16[1,2,208,384]{3,2,1,0:T(8,128)(2,1)S(1)}, bf16[1,2,208,384]{3,2,1,0:T(8,128)(2,1)S(1)}, u32[]{:S(2)}, u32[]{:S(2)}) collective-permute-start(bf16[1,2,208,384]{3,2,1,0:T(8,128)(2,1)S(1)} %bitcast.228), channel_id=1, source_target_pairs={{0,8},{4,12},{8,0},{12,4},{16,24},{20,28},{24,16},{28,20},{1,9},{5... | collective-permute-start | bytes 958472 | tf_op jit(solution)/shard_map/ppermute | solution.py:22
  417.3 20.8 %collective-permute-start.64 = (bf16[2,2,192,384]{3,2,1,0:T(8,128)(2,1)S(1)}, bf16[2,2,192,384]{3,2,1,0:T(8,128)(2,1)S(1)}, u32[]{:S(2)}, u32[]{:S(2)}) collective-permute-start(bf16[2,2,192,384]{3,2,1,0:T(8,128)(2,1)S(1)} %pad_maximum_fusion.4.near), channel_id=1, source_target_pairs={{0,4},{4,0},{8,12},{12,8},{16,20},{20,16},{24,28},{28,24},{1,5},{5... | collective-permute-start | bytes 1769480 | tf_op jit(solution)/shard_map/ppermute | solution.py:22
  418.9 31.9 %collective-permute-start.62 = (bf16[2,2,192,384]{3,2,1,0:T(8,128)(2,1)S(1)}, bf16[2,2,192,384]{3,2,1,0:T(8,128)(2,1)S(1)}, u32[]{:S(2)}, u32[]{:S(2)}) collective-permute-start(bf16[2,2,192,384]{3,2,1,0:T(8,128)(2,1)S(1)} %pad_maximum_fusion.5.near), channel_id=1, source_target_pairs={{0,4},{4,0},{8,12},{12,8},{16,20},{20,16},{24,28},{28,24},{1,5},{5... | collective-permute-start | bytes 1769480 | tf_op jit(solution)/shard_map/ppermute | solution.py:22
  425.5 37.9 %collective-permute-start.65 = (bf16[2,2,192,384]{3,2,1,0:T(8,128)(2,1)S(1)}, bf16[2,2,192,384]{3,2,1,0:T(8,128)(2,1)S(1)}, u32[]{:S(2)}, u32[]{:S(2)}) collective-permute-start(bf16[2,2,192,384]{3,2,1,0:T(8,128)(2,1)S(1)} %pad_maximum_fusion.6.near), channel_id=1, source_target_pairs={{0,4},{4,0},{8,12},{12,8},{16,20},{20,16},{24,28},{28,24},{1,5},{5... | collective-permute-start | bytes 1769480 | tf_op jit(solution)/shard_map/ppermute | solution.py:22
  427.2 40.7 %collective-permute-start.63 = (bf16[2,2,192,384]{3,2,1,0:T(8,128)(2,1)S(1)}, bf16[2,2,192,384]{3,2,1,0:T(8,128)(2,1)S(1)}, u32[]{:S(2)}, u32[]{:S(2)}) collective-permute-start(bf16[2,2,192,384]{3,2,1,0:T(8,128)(2,1)S(1)} %pad_maximum_fusion.7.near), channel_id=1, source_target_pairs={{0,8},{4,12},{8,0},{12,4},{16,24},{20,28},{24,16},{28,20},{1,9},{5... | collective-permute-start | bytes 1769480 | tf_op jit(solution)/shard_map/ppermute | solution.py:22
  429.1 45.2 %collective-permute-start.61 = (bf16[2,2,208,384]{3,2,1,0:T(8,128)(2,1)S(1)}, bf16[2,2,208,384]{3,2,1,0:T(8,128)(2,1)S(1)}, u32[]{:S(2)}, u32[]{:S(2)}) collective-permute-start(bf16[2,2,208,384]{3,2,1,0:T(8,128)(2,1)S(1)} %pad_maximum_fusion.near), channel_id=1, source_target_pairs={{0,4},{4,0},{8,12},{12,8},{16,20},{20,16},{24,28},{28,24},{1,5},{5... | collective-permute-start | bytes 1916936 | tf_op jit(solution)/shard_map/ppermute | solution.py:22
  (44 other events, 408.7 us)
where the time goes:
time: 489 us; the launch traced here: 479 us
  waiting for transfers between devices  242 us (49%)
  Pallas kernels  129 us (26%)
  starting transfers between devices  70.2 us (14%)
  local copies, waits for them, and re-layouts  22.9 us (5%)
  other arithmetic  12.4 us (3%)
    ppermute x64, waiting for transfers between devices, swap(): return lax.ppermute(value, axis, [(i, i ^ bit) for i in range(count)])  235 us
    pallas_call x17, Pallas kernels, call(): pl.pallas_call(kernel, name=name, in_specs=in_specs, out_specs=out_specs,...  129 us
    ppermute x64, starting transfers between devices, swap(): return lax.ppermute(value, axis, [(i, i ^ bit) for i in range(count)])  68.3 us
    unnamed x89, local copies, waits for them, and re-layouts  11.3 us
  transfers between devices with their start and end apart: 67, of which 41 were waited for; matrix products, arithmetic and copies ran while one was open for 5% of the time, Pallas kernels for 14%

commit v1 on v0

--- a/solution.py
+++ b/solution.py
@@ -266,29 +266,26 @@
     finish(waits)
 
 
-def in_bwd_kernel(layer, way, ids, d_ffn, d_resid_two, unit_one, inverse_one, small, slope_in, *rest):
+def in_bwd_kernel(layer, way, ids, d_ffn, d_resid_two, unit_one, inverse_one, slope, small, *rest):
     weights, rest = rest[:10], rest[10:]
     d_resid, small_grads, in_bias_grad, kept, sent = rest[:5]
-    w_in, w_out, d_pre, normed_t, slope, stage, sems, out_sems, slope_sem = rest[5:]
+    w_in, w_out, d_pre, normed_t, stage, sems, out_sems = rest[5:]
     in_copies, out_copies = ffn_copies(layer, ids, weights, w_in, w_out, sems)
-    slope_copy = pltpu.make_async_copy(slope_in, slope, slope_sem.at[0])
-    begin(out_copies[:2] + [slope_copy] + out_copies[2:] + in_copies)
+    begin(out_copies)
+    begin(in_copies)
     normed = unit_one[...] * small[layer, 3:4, :] + small[layer, 4:5, :]
     normed_t[...] = normed.astype(low).T
+    finish(out_copies)
     tile = w_in.shape[1] // 8
     going = []
-    slope_copy.wait()
-    for turn in range(8):
-        if turn % 2 == 0:
-            finish(([out_copies[0]], [out_copies[1]], out_copies[2:4], out_copies[4:6])[turn // 2])
-        t = 2 * ids[turn // 2] + turn % 2
-        columns = pl.ds(pl.multiple_of(t * tile, tile), tile)
+    for t in range(8):
+        columns = slice(t * tile, (t + 1) * tile)
         d_hidden = dot_nt(d_ffn[...], w_out[columns, :])
         d_tile = (d_hidden * slope[:, columns]).astype(low)
         d_pre[:, columns] = d_tile
         in_bias_grad[:, columns] = jnp.sum(d_tile.astype(f32), axis=0, keepdims=True)
         store_rows(stage, ids, dot(normed_t[...], d_tile), t, way)
-        going += piece_copies(stage, ids, t, way, kept, sent, out_sems, turn)
+        going += piece_copies(stage, ids, t, way, kept, sent, out_sems, t)
     finish(in_copies)
     d_normed = d_resid_two[...] + dot_nt(d_pre[...], w_in[...])
     unit = unit_one[...]
@@ -441,7 +438,7 @@
         input_output_aliases=dict(aliases),
         compiler_params=pltpu.CompilerParams(vmem_limit_bytes=VMEM_BYTES),
         cost_estimate=pl.CostEstimate(
-            flops=int(time * 0.22e9), bytes_accessed=int(time * 0.72e6), transcendentals=0
+            flops=int(time * 1.1e9), bytes_accessed=int(time * 3.6e6), transcendentals=0
         ),
     )(*args)
 
@@ -463,18 +460,11 @@
 
 
 class Order:
-    def __init__(self):
-        self.last = None
-
-    def after(self, values):
-        if self.last is None:
-            return values
-        values, self.last = lax.optimization_barrier((values, self.last))
-        return values
+    def __init__(self, ids):
+        self.ids = ids
 
     def wait(self, values):
-        values = self.after(values)
-        self.last = values
+        values, self.ids = lax.optimization_barrier((values, self.ids))
         return values
 
 
@@ -490,31 +480,25 @@
         self.stage = 0
 
     def step(self, order):
-        received = order.after(self.flying)
+        received = order.wait(self.flying)
         stage, way = self.stage, self.way
         if stage < len(way):
-            send = added(self.kept[1], received[1])
+            send = order.wait(added(self.kept[1], received[1]))
             self.kept = added(self.kept[0], received[0])
             self.flying = swap(send, *STEPS[way[stage]])
-            order.last = send
         elif stage < len(way) + 1 + len(self.back):
             if stage == len(way):
                 piece = added(self.kept, received)
-                if not self.rest:
-                    self.block = piece[None]
-            elif stage == len(way) + 1 and self.rest:
-                piece = added(self.kept, received)
-                for bit in self.rest[1:]:
+                for bit in self.rest[:-1]:
                     piece = added(piece, swap(piece, "wide", bit))
-                self.block = piece[None]
+                self.kept = order.wait(piece)
+                self.flying = swap(self.kept, "wide", self.rest[-1])
             else:
-                self.block = jnp.concatenate([self.block, received], axis=0)
-                piece = self.block
-            order.last = piece
-            if stage == len(way) and self.rest:
-                self.kept = piece
-                self.flying = swap(piece, "wide", self.rest[0])
-            else:
+                if stage == len(way) + 1:
+                    self.block = added(self.kept, received)[None]
+                else:
+                    self.block = jnp.concatenate([self.block, received], axis=0)
+                self.block = order.wait(self.block)
                 self.flying = swap(self.block, *STEPS[self.back[stage - len(way) - 1]])
         else:
             self.far = received
@@ -547,14 +531,14 @@
     layers, share, ffn = in_weight.shape
     ffn_share = out_weight.shape[1]
     wide_count = lax.axis_size("wide")
-    assert wide_count & (wide_count - 1) == 0 and wide_count >= 1 << HALVINGS and lax.axis_size("narrow") == 4
+    assert wide_count & (wide_count - 1) == 0 and wide_count > 1 << HALVINGS and lax.axis_size("narrow") == 4
     tile = ffn // 8
     me = lax.axis_index("narrow").astype(jnp.int32)
     wide_me = lax.axis_index("wide").astype(jnp.int32)
     y = wide_me & 1
     ids = jnp.stack([me, me ^ 1, me ^ 2, me ^ 3, y, wide_me & (2**HALVINGS - 1)])
 
-    order = Order()
+    order = Order(ids)
 
     def half_of(weight, layer):
         rows = weight.shape[1] // 2
@@ -581,55 +565,53 @@
         swapped = (me & bit) != 0
         return jnp.stack([jnp.where(swapped, high_one, low_one), jnp.where(swapped, low_one, high_one)])
 
-    near_x[0] = swap(halves[0], "narrow", 2)
-    order.last = halves[0]
-    core[0], core[1] = swap(own[0], "narrow", 1), swap(own[1], "narrow", 1)
-    short = order.after((q_bias, v_bias, o_bias, norm1_gain, norm1_bias, out_bias, norm2_gain, norm2_bias))
+    def send_x(*which):
+        for i in which:
+            near_x[i] = swap(order.wait(halves[i]), "narrow", 2)
+
+    def send_core(i):
+        core[i] = swap(order.wait(own[i]), "narrow", 1)
+
+    def arrive(*events):
+        for kind, i in events:
+            if kind == "x":
+                near_x[i] = order.wait(near_x[i])
+                far_x[i] = swap(near_x[i], "wide", 1)
+            elif kind == "y":
+                far_x[i] = order.wait(far_x[i])
+                diagonal[i] = swap(order.wait(jnp.concatenate([near_x[i], far_x[i]], axis=0)), "narrow", 1)
+            elif kind == "d":
+                diagonal[i] = order.wait(diagonal[i])
+            else:
+                core[i] = order.wait(core[i])
+
+    send_x(0)
+    short = order.wait((q_bias, v_bias, o_bias, norm1_gain, norm1_bias, out_bias, norm2_gain, norm2_bias))
     packed = call(
         pack_kernel, "pack", 1, [VMEM] * 9, VMEM, shape((layers, 12, share), f32), [], tuple(short) + (in_bias,)
     )
-    halves[1:], packed = order.wait((halves[1:], packed))
-    near_x[0], core[0], core[1] = order.wait((near_x[0], core[0], core[1]))
-
-    others = [
-        lax.ppermute(order.after(packed), "narrow", [(i, i ^ away) for i in range(4)]) for away in (1, 2, 3)
-    ]
-    far_x[0] = swap(near_x[0], "wide", 1)
-    near_x[1] = swap(order.after(halves[1]), "narrow", 2)
-    far_x[0], near_x[1], others = order.wait((far_x[0], near_x[1], others))
+    packed = order.wait(packed)
+    others = [lax.ppermute(packed, "narrow", [(i, i ^ away) for i in range(4)]) for away in (1, 2, 3)]
+    send_x(1)
+    halves[2:] = order.wait(halves[2:])
+    others[0] = order.wait(others[0])
+    send_core(0)
+    arrive(("x", 0))
+    others[1:] = order.wait(others[1:])
+    send_x(2)
+    send_core(1)
     packed = in_order(in_order(packed, others[0], 1), in_order(others[1], others[2], 1), 2)
     packed = packed.reshape(4, layers, 12, share)
     small = packed[:, :, :8].transpose(1, 2, 0, 3).reshape(layers, 8, width)
     full_in_bias = packed[:, :, 8:].transpose(1, 0, 2, 3).reshape(layers, 1, ffn)
-
-    def join(i):
-        both = jnp.concatenate([near_x[i], far_x[i]], axis=0)
-        diagonal[i] = swap(both, "narrow", 1)
-        return both
-
-    def begin_round(i):
-        both = join(i)
-        if i + 1 < len(halves):
-            far_x[i + 1] = swap(near_x[i + 1], "wide", 1)
-        if i + 2 < len(halves):
-            near_x[i + 2] = swap(order.after(halves[i + 2]), "narrow", 2)
-        order.last = both
-
-    def end_round(i):
-        if i + 2 < len(halves):
-            far_x[i + 1], near_x[i + 2] = order.wait((far_x[i + 1], near_x[i + 2]))
-        elif i + 1 < len(halves):
-            far_x[i + 1] = order.wait(far_x[i + 1])
-
-    def arrive(i):
-        diagonal[i] = order.wait(diagonal[i])
-
-    begin_round(0)
-    core[2], core[3] = swap(order.after(own[2]), "narrow", 1), swap(order.after(own[3]), "narrow", 1)
-    ids, small, full_in_bias = order.wait((ids, small, full_in_bias))
-    arrive(0)
-    core[2], core[3] = order.wait((core[2], core[3]))
-    end_round(0)
+    small, full_in_bias = order.wait((small, full_in_bias))
+    arrive(("c", 0), ("x", 1))
+    send_x(3)
+    arrive(("c", 1))
+    send_core(2)
+    arrive(("y", 0), ("c", 2))
+    send_core(3)
+    arrive(("d", 0))
 
     w_qkv = pltpu.VMEM((width, 3 * width), low)
     w_o = pltpu.VMEM((width, width), low)
@@ -648,8 +630,13 @@
     def stage(rows):
         return pltpu.VMEM((2, 2, 2, 2, 2, rows, tile), low)
 
+    def tie(outs, which):
+        outs = list(outs)
+        outs[which] = order.wait(outs[which])
+        return outs
+
     def attn_forward(layer, x):
-        x = order.after(x)
+        x = order.wait(x)
         outs = call(
             functools.partial(attn_fwd_kernel, layer),
             "attn_fwd",
@@ -658,13 +645,12 @@
             [VMEM] * 5,
             [shape((tokens, 3 * width), low), shape((HEADS, tokens, tokens), low), rows_low, rows_f32, column_f32],
             [w_qkv, w_o, pltpu.VMEM((tokens, tokens), f32), copy_sems],
-            (ids, lengths, x, cell_ids, small) + attn_weights(layer),
+            (order.ids, lengths, x, cell_ids, small) + attn_weights(layer),
         )
-        order.last = outs[-1]
-        return outs
+        return tie(outs, 3)
 
     def ffn_forward(layer, unit_one):
-        unit_one = order.after(unit_one)
+        unit_one = order.wait(unit_one)
         outs = call(
             functools.partial(ffn_fwd_kernel, layer),
             "ffn_fwd",
@@ -681,13 +667,12 @@
                 copy_sems,
                 piece_sems,
             ],
-            (ids, unit_one, full_in_bias, small) + ffn_weights(layer),
+            (order.ids, unit_one, full_in_bias, small) + ffn_weights(layer),
         )
-        order.last = outs[-2]
-        return outs
+        return tie(outs, 4)
 
     def out_backward(layer, way, grad, unit_two, inverse_two, hidden):
-        grad = order.after(grad)
+        grad = order.wait(grad)
         outs = call(
             functools.partial(out_bwd_kernel, layer, way),
             "out_bwd",
@@ -696,18 +681,17 @@
             [VMEM] * 3 + [ANY] * 2,
             [rows_low, rows_f32, eight_f32] + pieces(share),
             [stage(share), pltpu.SemaphoreType.DMA((4,))],
-            (ids, grad, unit_two, inverse_two, hidden, small),
+            (order.ids, grad, unit_two, inverse_two, hidden, small),
         )
-        order.last = outs[2]
-        return outs
+        return tie(outs, 0)
 
     def in_backward(layer, way, d_ffn, d_resid_two, unit_one, inverse_one, slope):
-        d_ffn = order.after(d_ffn)
+        d_ffn = order.wait(d_ffn)
         outs = call(
             functools.partial(in_bwd_kernel, layer, way),
             "in_bwd",
             14,
-            [SMEM] + [VMEM] * 5 + [ANY] * 11,
+            [SMEM] + [VMEM] * 6 + [ANY] * 10,
             [VMEM] * 3 + [ANY] * 2,
             [rows_f32, eight_f32, shape((1, ffn), f32)] + pieces(share),
             [
@@ -715,19 +699,16 @@
                 w_out,
                 pltpu.VMEM((tokens, ffn), low),
                 pltpu.VMEM((width, tokens), low),
-                pltpu.VMEM((tokens, ffn), f32),
                 stage(share),
                 copy_sems,
                 piece_sems,
-                pltpu.SemaphoreType.DMA((1,)),
             ],
-            (ids, d_ffn, d_resid_two, unit_one, inverse_one, small, slope) + ffn_weights(layer),
+            (order.ids, d_ffn, d_resid_two, unit_one, inverse_one, slope, small) + ffn_weights(layer),
         )
-        order.last = outs[1]
-        return outs
+        return tie(outs, 0)
 
     def attn_backward(layer, way, d_resid, x, qkv_rows, probs, context, small_others):
-        d_resid = order.after(d_resid)
+        d_resid = order.wait(d_resid)
         rows = share + (SMALL_ROWS if small_others else 0)
         outs = call(
             functools.partial(attn_bwd_kernel, layer, way),
@@ -747,10 +728,9 @@
                 copy_sems,
                 piece_sems,
             ],
-            (ids, d_resid, x, qkv_rows, probs, context) + attn_weights(layer) + tuple(small_others),
+            (order.ids, d_resid, x, qkv_rows, probs, context) + attn_weights(layer) + tuple(small_others),
         )
-        order.last = outs[1]
-        return outs
+        return tie(outs, 0)
 
     def unpack(layer, name, slab, earlier):
         dims = {
@@ -760,7 +740,7 @@
         }[name]
         last = name == "attn" and layer == 0
         extra = [(layers, share)] * 8 + [(layers, ffn_share)] if last else [(8, 128)]
-        near, far = order.after((slab.block, slab.far))
+        near, far = order.wait((slab.block, slab.far))
         rows = near.shape[2]
         outs = call(
             functools.partial(unpack_kernel, layer, name, slab.back, len(earlier)),
@@ -775,29 +755,21 @@
                 pltpu.SemaphoreType.DMA((8,)),
                 pltpu.SemaphoreType.DMA((8,)),
             ],
-            (ids, near, far, *earlier),
+            (order.ids, near, far, *earlier),
             {3 + i: i for i in range(len(earlier))},
         )
-        order.last = outs[-1]
-        return tuple(outs)
-
-    begin_round(1)
+        return tuple(tie(outs, 0))
+
     first_attn = attn_forward(0, tables_in)
-    arrive(1)
-    end_round(1)
-    begin_round(2)
-    arrive(2)
+    arrive(("x", 2))
+    send_x(4)
+    arrive(("y", 1), ("c", 3), ("d", 1), ("x", 3))
+    send_x(5)
+    arrive(("y", 2), ("d", 2))
     first_ffn = ffn_forward(0, first_attn[3])
-    end_round(2)
-    begin_round(3)
-    arrive(3)
+    arrive(("x", 4), ("y", 3), ("d", 3))
     second_attn = attn_forward(1, first_ffn[4])
-    end_round(3)
-    begin_round(4)
-    arrive(4)
-    end_round(4)
-    begin_round(5)
-    arrive(5)
+    arrive(("x", 5), ("y", 4), ("y", 5), ("d", 4), ("d", 5))
     second_ffn = ffn_forward(1, second_attn[3])
     mixed_out = second_ffn[4]
     inputs = (tables_in, first_ffn[4])

time: 489 us -> 486 us (level)
  other arithmetic: 12.4 us -> 19 us
    ppermute x3, waiting for transfers between devices: 7.82 us -> 1.51 us  [body(): lax.ppermute(packed, 'narrow', [(i, i ^ away) for i in range(4)])]
    convert_element_type x30 -> x24, other arithmetic: 9.33 us -> 14.9 us  [added(): return (a.astype(f32) + b.astype(f32)).astype(low)]
    unnamed x89 -> x81, local copies, waits for them, and re-layouts: 11.3 us -> 15.8 us
  transfers between devices with their start and end apart: 67 -> 67, of which waited for: 41 -> 36; matrix products, arithmetic and copies ran while one was open for 5% -> 5% of each run, Pallas kernels for 14% -> 14%
where the time goes in v1:
time: 486 us; the launch traced here: 477 us
  waiting for transfers between devices  238 us (49%)
  Pallas kernels  126 us (26%)
  starting transfers between devices  65.9 us (14%)
  local copies, waits for them, and re-layouts  25.6 us (5%)
  other arithmetic  19 us (4%)
    ppermute x64, waiting for transfers between devices, swap(): return lax.ppermute(value, axis, [(i, i ^ bit) for i in range(count)])  237 us
    pallas_call x17, Pallas kernels, call(): pl.pallas_call(kernel, name=name, in_specs=in_specs, out_specs=out_specs,...  126 us
    ppermute x64, starting transfers between devices, swap(): return lax.ppermute(value, axis, [(i, i ^ bit) for i in range(count)])  64.1 us
    unnamed x81, local copies, waits for them, and re-layouts  15.8 us
    convert_element_type x24, other arithmetic, added(): return (a.astype(f32) + b.astype(f32)).astype(low)  14.9 us
  transfers between devices with their start and end apart: 67, of which 36 were waited for; matrix products, arithmetic and copies ran while one was open for 5% of the time, Pallas kernels for 14%

profile of v1, /device:TPU:0, one launch (start us, length us, event | category | flops | bytes accessed | tf_op | source)
XLA Modules:
  0.0 476.5 jit_solution(15311331685463507217)
XLA Ops:
  10.0 2.9 collective-permute-start
  15.7 11.5 %collective-permute-done.rest_4_ = bf16[96,3072]{1,0:T(8,128)(2,1)S(1)} collective-permute-done((bf16[96,3072]{1,0:T(8,128)(2,1)}, bf16[96,3072]{1,0:T(8,128)(2,1)S(1)}, u32[]{:S(2)}, u32[]{:S(2)}) %collective-permute-start) | collective-permute-done | bytes 589856 | tf_op jit(solution)/shard_map/ppermute | solution.py:22
  33.8 1.5 reshape.386.small
  35.4 5.3 %collective-permute-done.6.rest_2_ = bf16[96,3072]{1,0:T(8,128)(2,1)S(1)} collective-permute-done((bf16[96,3072]{1,0:T(8,128)(2,1)S(1)}, bf16[96,3072]{1,0:T(8,128)(2,1)S(1)}, u32[]{:S(2)}, u32[]{:S(2)}) %collective-permute-start.6) | collective-permute-done | bytes 589856 | tf_op jit(solution)/shard_map/ppermute | solution.py:22
  40.6 1.8 collective-permute-start.2
  42.5 13.9 %collective-permute-done.2.rest_5_ = bf16[96,3072]{1,0:T(8,128)(2,1)S(1)} collective-permute-done((bf16[96,3072]{1,0:T(8,128)(2,1)S(1)}, bf16[96,3072]{1,0:T(8,128)(2,1)S(1)}, u32[]{:S(2)}, u32[]{:S(2)}) %collective-permute-start.2) | collective-permute-done | bytes 589856 | tf_op jit(solution)/shard_map/ppermute | solution.py:22
  57.9 1.8 collective-permute-start.10
  59.7 1.5 collective-permute-start.13
  62.3 8.2 %attn_fwd.2 = (bf16[256,2304]{1,0:T(8,128)(2,1)}, bf16[12,256,256]{2,1,0:T(8,128)(2,1)}, bf16[256,768]{1,0:T(8,128)(2,1)}, f32[256,768]{1,0:T(8,128)}, f32[256,1]{1,0:T(8,128)}) custom-call(s32[6]{0:T(128)} %stack.50.ids, s32[1]{0:T(128)S(6)} %copy.47.length, bf16[256,768]{1,0:T(8,128)(2,1)} %x.2, s32[1,256]{1,0:T(1,128)} %cell_row.3, ...), custom_call_target="tpu_custom_call" | custom-call | flops 14300000256 | bytes 46800000 | tf_op jit(solution)/shard_map/attn_fwd/pallas_call | solution.py:431
  70.5 3.3 collective-permute-done.10.rest_7_
  76.5 1.6 collective-permute-start.11
  78.8 12.9 %collective-permute-done.12.rest_4_ = bf16[96,3072]{1,0:T(8,128)(2,1)S(1)} collective-permute-done((bf16[96,3072]{1,0:T(8,128)(2,1)S(1)}, bf16[96,3072]{1,0:T(8,128)(2,1)S(1)}, u32[]{:S(2)}, u32[]{:S(2)}) %collective-permute-start.12) | collective-permute-done | bytes 589856 | tf_op jit(solution)/shard_map/ppermute | solution.py:22
  92.8 1.6 collective-permute-start.18
  96.9 10.6 %ffn_fwd.2 = (bf16[256,3072]{1,0:T(8,128)(2,1)}, f32[256,3072]{1,0:T(8,128)}, f32[256,768]{1,0:T(8,128)}, f32[256,1]{1,0:T(8,128)}, bf16[256,768]{1,0:T(8,128)(2,1)}) custom-call(s32[6]{0:T(128)} %stack.50.ids, f32[256,768]{1,0:T(8,128)} %get-tuple-element.476.unit_one, f32[2,1,3072]{2,1,0:T(1,128)} %reshape.387.in_bias, f32[2,8,768]{2,1,0:T(8,128)} %reshape.386.small, ...), custom_call_target="tpu_custom_call" | custom-call | flops 11000000512 | bytes 36000000 | tf_op jit(solution)/shard_map/ffn_fwd/pallas_call | solution.py:431
  111.5 1.6 collective-permute-start.22
  114.5 8.1 %attn_fwd.3 = (bf16[256,2304]{1,0:T(8,128)(2,1)}, bf16[12,256,256]{2,1,0:T(8,128)(2,1)}, bf16[256,768]{1,0:T(8,128)(2,1)}, f32[256,768]{1,0:T(8,128)}, f32[256,1]{1,0:T(8,128)}) custom-call(s32[6]{0:T(128)} %stack.50.ids, s32[1]{0:T(128)S(6)} %copy.47.length, bf16[256,768]{1,0:T(8,128)(2,1)} %get-tuple-element.494.x, s32[1,256]{1,0:T(1,128)} %cell_row.3, ...), custom_call_target="tpu_custom_call" | custom-call | flops 14300000256 | bytes 46800000 | tf_op jit(solution)/shard_map/attn_fwd/pallas_call | solution.py:431
  122.6 4.2 collective-permute-done.20.rest_7_
  129.1 12.6 %collective-permute-done.21.rest_8_ = bf16[384,768]{1,0:T(8,128)(2,1)S(1)} collective-permute-done((bf16[384,768]{1,0:T(8,128)(2,1)S(1)}, bf16[384,768]{1,0:T(8,128)(2,1)S(1)}, u32[]{:S(2)}, u32[]{:S(2)}) %collective-permute-start.21) | collective-permute-done | bytes 589856 | tf_op jit(solution)/shard_map/ppermute | solution.py:22
  142.6 2.8 collective-permute-done.23.rest_9_
  146.5 10.7 %ffn_fwd.3 = (bf16[256,3072]{1,0:T(8,128)(2,1)}, f32[256,3072]{1,0:T(8,128)}, f32[256,768]{1,0:T(8,128)}, f32[256,1]{1,0:T(8,128)}, bf16[256,768]{1,0:T(8,128)(2,1)}) custom-call(s32[6]{0:T(128)} %stack.50.ids, f32[256,768]{1,0:T(8,128)} %get-tuple-element.514.unit_one, f32[2,1,3072]{2,1,0:T(1,128)} %reshape.387.in_bias, f32[2,8,768]{2,1,0:T(8,128)} %reshape.386.small, ...), custom_call_target="tpu_custom_call" | custom-call | flops 11000000512 | bytes 36000000 | tf_op jit(solution)/shard_map/ffn_fwd/pallas_call | solution.py:431
  157.1 6.1 %out_bwd.2 = (bf16[256,768]{1,0:T(8,128)(2,1)}, f32[256,768]{1,0:T(8,128)}, f32[8,768]{1,0:T(8,128)}, bf16[2,2,2,2,192,384]{5,4,3,2,1,0:T(8,128)(2,1)}, bf16[2,2,2,2,192,384]{5,4,3,2,1,0:T(8,128)(2,1)}) custom-call(s32[6]{0:T(128)} %stack.50.ids, bf16[256,768]{1,0:T(8,128)(2,1)} %grad, f32[256,768]{1,0:T(8,128)} %get-tuple-element.522.unit_two, ...), custom_call_target="tpu_custom_call" | custom-call | flops 8800000000 | bytes 28800000 | tf_op jit(solution)/shard_map/out_bwd/pallas_call | solution.py:431
  163.4 13.2 %in_bwd.2 = (f32[256,768]{1,0:T(8,128)}, f32[8,768]{1,0:T(8,128)}, f32[1,3072]{1,0:T(1,128)}, bf16[2,2,2,2,192,384]{5,4,3,2,1,0:T(8,128)(2,1)}, bf16[2,2,2,2,192,384]{5,4,3,2,1,0:T(8,128)(2,1)}) custom-call(s32[6]{0:T(128)} %stack.50.ids, bf16[256,768]{1,0:T(8,128)(2,1)} %get-tuple-element.527.d_ffn, f32[256,768]{1,0:T(8,128)} %get-tuple-element.528.d_resid_two, ...), custom_call_target="tpu_custom_call" | custom-call | flops 15399999488 | bytes 50400000 | tf_op jit(solution)/shard_map/in_bwd/pallas_call | solution.py:431
  177.7 3.7 collective-permute-done.25
  182.1 13.0 %attn_bwd.2 = (bf16[256,768]{1,0:T(8,128)(2,1)}, f32[8,768]{1,0:T(8,128)}, bf16[2,2,2,2,192,384]{5,4,3,2,1,0:T(8,128)(2,1)}, bf16[2,2,2,2,192,384]{5,4,3,2,1,0:T(8,128)(2,1)}) custom-call(s32[6]{0:T(128)} %stack.50.ids, f32[256,768]{1,0:T(8,128)} %get-tuple-element.545.d_resid, bf16[256,768]{1,0:T(8,128)(2,1)} %get-tuple-element.494.x, ...), custom_call_target="tpu_custom_call" | custom-call | flops 17600000000 | bytes 57600000 | tf_op jit(solution)/shard_map/attn_bwd/pallas_call | solution.py:431
  195.5 6.0 %out_bwd.3 = (bf16[256,768]{1,0:T(8,128)(2,1)}, f32[256,768]{1,0:T(8,128)}, f32[8,768]{1,0:T(8,128)}, bf16[2,2,2,2,192,384]{5,4,3,2,1,0:T(8,128)(2,1)}, bf16[2,2,2,2,192,384]{5,4,3,2,1,0:T(8,128)(2,1)}) custom-call(s32[6]{0:T(128)} %stack.50.ids, bf16[256,768]{1,0:T(8,128)(2,1)} %get-tuple-element.551.grad, f32[256,768]{1,0:T(8,128)} %get-tuple-element.552.unit_two, ...), custom_call_target="tpu_custom_call" | custom-call | flops 8800000000 | bytes 28800000 | tf_op jit(solution)/shard_map/out_bwd/pallas_call | solution.py:431
  202.2 1.6 collective-permute-start.30
  203.8 26.2 %collective-permute-done.27 = bf16[2,2,2,192,384]{4,3,2,1,0:T(8,128)(2,1)S(1)} collective-permute-done((bf16[2,2,2,192,384]{4,3,2,1,0:T(8,128)(2,1)S(1)}, bf16[2,2,2,192,384]{4,3,2,1,0:T(8,128)(2,1)S(1)}, u32[]{:S(2)}, u32[]{:S(2)}) %collective-permute-start.27) | collective-permute-done | bytes 1179680 | tf_op jit(solution)/shard_map/ppermute | solution.py:22
  230.4 1.6 collective-permute-start.28
  235.0 10.3 %collective-permute-done.28 = bf16[2,2,192,384]{3,2,1,0:T(8,128)(2,1)S(1)} collective-permute-done((bf16[2,2,192,384]{3,2,1,0:T(8,128)(2,1)S(1)}, bf16[2,2,192,384]{3,2,1,0:T(8,128)(2,1)S(1)}, u32[]{:S(2)}, u32[]{:S(2)}) %collective-permute-start.28) | collective-permute-done | bytes 589856 | tf_op jit(solution)/shard_map/ppermute | solution.py:22
  245.4 1.5 collective-permute-start.32
  247.7 5.3 %collective-permute-done.32 = bf16[2,192,384]{2,1,0:T(8,128)(2,1)S(1)} collective-permute-done((bf16[2,192,384]{2,1,0:T(8,128)(2,1)S(1)}, bf16[2,192,384]{2,1,0:T(8,128)(2,1)S(1)}, u32[]{:S(2)}, u32[]{:S(2)}) %collective-permute-start.32) | collective-permute-done | bytes 294944 | tf_op jit(solution)/shard_map/ppermute | solution.py:22
  253.2 12.8 %in_bwd.3 = (f32[256,768]{1,0:T(8,128)}, f32[8,768]{1,0:T(8,128)}, f32[1,3072]{1,0:T(1,128)}, bf16[2,2,2,2,192,384]{5,4,3,2,1,0:T(8,128)(2,1)}, bf16[2,2,2,2,192,384]{5,4,3,2,1,0:T(8,128)(2,1)}) custom-call(s32[6]{0:T(128)} %stack.50.ids, bf16[256,768]{1,0:T(8,128)(2,1)} %get-tuple-element.589.d_ffn, f32[256,768]{1,0:T(8,128)} %get-tuple-element.590.d_resid_two, ...), custom_call_target="tpu_custom_call" | custom-call | flops 15399999488 | bytes 50400000 | tf_op jit(solution)/shard_map/in_bwd/pallas_call | solution.py:431
  267.6 2.6 collective-permute-start.35
  271.5 23.5 %collective-permute-done.36 = bf16[2,2,2,192,384]{4,3,2,1,0:T(8,128)(2,1)S(1)} collective-permute-done((bf16[2,2,2,192,384]{4,3,2,1,0:T(8,128)(2,1)S(1)}, bf16[2,2,2,192,384]{4,3,2,1,0:T(8,128)(2,1)S(1)}, u32[]{:S(2)}, u32[]{:S(2)}) %collective-permute-start.36) | collective-permute-done | bytes 1179680 | tf_op jit(solution)/shard_map/ppermute | solution.py:22
  297.6 1.7 add_convert_fusion.2
  300.9 3.4 collective-permute-done.37
  305.6 12.9 %attn_bwd.3 = (bf16[256,768]{1,0:T(8,128)(2,1)}, f32[8,768]{1,0:T(8,128)}, bf16[2,2,2,2,208,384]{5,4,3,2,1,0:T(8,128)(2,1)}, bf16[2,2,2,2,208,384]{5,4,3,2,1,0:T(8,128)(2,1)}) custom-call(s32[6]{0:T(128)} %stack.50.ids, f32[256,768]{1,0:T(8,128)} %get-tuple-element.622.d_resid, bf16[256,768]{1,0:T(8,128)(2,1)} %x.2, ...), custom_call_target="tpu_custom_call" | custom-call | flops 17600000000 | bytes 57600000 | tf_op jit(solution)/shard_map/attn_bwd/pallas_call | solution.py:431
  320.4 2.6 collective-permute-start.41
  323.0 1.6 collective-permute-start.46
  324.6 9.7 %collective-permute-done.43.far = bf16[2,2,192,384]{3,2,1,0:T(8,128)(2,1)S(1)} collective-permute-done((bf16[2,2,192,384]{3,2,1,0:T(8,128)(2,1)S(1)}, bf16[2,2,192,384]{3,2,1,0:T(8,128)(2,1)S(1)}, u32[]{:S(2)}, u32[]{:S(2)}) %collective-permute-start.43) | collective-permute-done | bytes 589856 | tf_op jit(solution)/shard_map/ppermute | solution.py:22
  335.4 3.9 unpack.6
  340.4 1.7 collective-permute-start.51
  345.0 10.9 %collective-permute-done.45 = bf16[2,192,384]{2,1,0:T(8,128)(2,1)S(1)} collective-permute-done((bf16[2,192,384]{2,1,0:T(8,128)(2,1)S(1)}, bf16[2,192,384]{2,1,0:T(8,128)(2,1)S(1)}, u32[]{:S(2)}, u32[]{:S(2)}) %collective-permute-start.45) | collective-permute-done | bytes 294944 | tf_op jit(solution)/shard_map/ppermute | solution.py:22
  356.9 6.2 %collective-permute-done.48 = bf16[2,2,2,192,384]{4,3,2,1,0:T(8,128)(2,1)} collective-permute-done((bf16[2,2,2,192,384]{4,3,2,1,0:T(8,128)(2,1)}, bf16[2,2,2,192,384]{4,3,2,1,0:T(8,128)(2,1)}, u32[]{:S(2)}, u32[]{:S(2)}) %collective-permute-start.48) | collective-permute-done | bytes 1179680 | tf_op jit(solution)/shard_map/ppermute | solution.py:22
  363.4 1.5 fusion.26
  364.9 1.5 collective-permute-start.49
  367.1 2.6 collective-permute-start.47
  371.2 16.3 %collective-permute-done.50 = bf16[2,192,384]{2,1,0:T(8,128)(2,1)S(1)} collective-permute-done((bf16[2,192,384]{2,1,0:T(8,128)(2,1)S(1)}, bf16[2,192,384]{2,1,0:T(8,128)(2,1)S(1)}, u32[]{:S(2)}, u32[]{:S(2)}) %collective-permute-start.50) | collective-permute-done | bytes 294944 | tf_op jit(solution)/shard_map/ppermute | solution.py:22
  388.6 2.6 collective-permute-start.55
  391.4 1.6 collective-permute-start.56
  394.1 12.9 %collective-permute-done.56 = bf16[2,192,384]{2,1,0:T(8,128)(2,1)S(1)} collective-permute-done((bf16[2,192,384]{2,1,0:T(8,128)(2,1)S(1)}, bf16[2,192,384]{2,1,0:T(8,128)(2,1)S(1)}, u32[]{:S(2)}, u32[]{:S(2)}) %collective-permute-start.56) | collective-permute-done | bytes 294944 | tf_op jit(solution)/shard_map/ppermute | solution.py:22
  409.4 3.0 collective-permute-start.58
  412.5 3.7 unpack.7
  416.8 7.7 %collective-permute-done.52 = bf16[2,2,208,384]{3,2,1,0:T(8,128)(2,1)S(1)} collective-permute-done((bf16[2,2,208,384]{3,2,1,0:T(8,128)(2,1)S(1)}, bf16[2,2,208,384]{3,2,1,0:T(8,128)(2,1)S(1)}, u32[]{:S(2)}, u32[]{:S(2)}) %collective-permute-start.52) | collective-permute-done | bytes 639008 | tf_op jit(solution)/shard_map/ppermute | solution.py:22
  425.4 1.6 collective-permute-start.64
  427.5 7.5 %collective-permute-done.57 = bf16[2,208,384]{2,1,0:T(8,128)(2,1)S(1)} collective-permute-done((bf16[2,208,384]{2,1,0:T(8,128)(2,1)S(1)}, bf16[2,208,384]{2,1,0:T(8,128)(2,1)S(1)}, u32[]{:S(2)}, u32[]{:S(2)}) %collective-permute-start.57) | collective-permute-done | bytes 319520 | tf_op jit(solution)/shard_map/ppermute | solution.py:22
  438.0 3.7 unpack.8
  441.7 6.4 %collective-permute-done.61.far = bf16[2,2,192,384]{3,2,1,0:T(8,128)(2,1)S(1)} collective-permute-done((bf16[2,2,192,384]{3,2,1,0:T(8,128)(2,1)S(1)}, bf16[2,2,192,384]{3,2,1,0:T(8,128)(2,1)S(1)}, u32[]{:S(2)}, u32[]{:S(2)}) %collective-permute-start.61) | collective-permute-done | bytes 589856 | tf_op jit(solution)/shard_map/ppermute | solution.py:22
  449.0 3.7 unpack.9
  453.0 2.1 collective-permute-start.66
  455.1 5.7 %collective-permute-done.63 = bf16[1,2,208,384]{3,2,1,0:T(8,128)(2,1)S(1)} collective-permute-done((bf16[1,2,208,384]{3,2,1,0:T(8,128)(2,1)S(1)}, bf16[1,2,208,384]{3,2,1,0:T(8,128)(2,1)S(1)}, u32[]{:S(2)}, u32[]{:S(2)}) %collective-permute-start.63) | collective-permute-done | bytes 319520 | tf_op jit(solution)/shard_map/ppermute | solution.py:22
  462.0 5.1 %collective-permute-done.66.far = bf16[2,2,192,384]{3,2,1,0:T(8,128)(2,1)S(1)} collective-permute-done((bf16[2,2,192,384]{3,2,1,0:T(8,128)(2,1)S(1)}, bf16[2,2,192,384]{3,2,1,0:T(8,128)(2,1)S(1)}, u32[]{:S(2)}, u32[]{:S(2)}) %collective-permute-start.66) | collective-permute-done | bytes 589856 | tf_op jit(solution)/shard_map/ppermute | solution.py:22
  467.9 3.7 unpack.10
  472.5 3.8 unpack.11
  (224 shorter events, 76.8 us)
Async XLA Ops:
  6.2 3.1 collective-permute-start.1
  9.9 25.5 %collective-permute-start.7 = (bf16[2,192,2304]{2,1,0:T(8,128)(2,1)}, bf16[2,192,2304]{2,1,0:T(8,128)(2,1)}, u32[]{:S(2)}, u32[]{:S(2)}) collective-permute-start(bf16[2,192,2304]{2,1,0:T(8,128)(2,1)} %rest_0_.15), channel_id=1, source_target_pairs={{0,1},{1,0},{2,3},{3,2},{4,5},{5,4},{6,7},{7,6},{8,9},{9,8},{10,11... | collective-permute-start | bytes 5308424 | tf_op jit(solution)/shard_map/ppermute | solution.py:22
  10.0 17.3 %collective-permute-start = (bf16[96,3072]{1,0:T(8,128)(2,1)}, bf16[96,3072]{1,0:T(8,128)(2,1)S(1)}, u32[]{:S(2)}, u32[]{:S(2)}) collective-permute-start(bf16[96,3072]{1,0:T(8,128)(2,1)} %get-tuple-element.400), channel_id=1, source_target_pairs={{0,2},{1,3},{2,0},{3,1},{4,6},{5,7},{6,4},{7,5},{8,10},{9,11},{10,... | collective-permute-start | bytes 1769480 | tf_op jit(solution)/shard_map/ppermute | solution.py:22
  12.9 14.7 %collective-permute-start.4 = (f32[2,12,192]{2,1,0:T(8,128)}, f32[2,12,192]{2,1,0:T(8,128)}, u32[]{:S(2)}, u32[]{:S(2)}) collective-permute-start(f32[2,12,192]{2,1,0:T(8,128)} %pack.1), channel_id=1, source_target_pairs={{0,3},{1,2},{2,1},{3,0},{4,7},{5,6},{6,5},{7,4},{8,11},{9,10},{10,... | collective-permute-start | bytes 55304 | tf_op jit(solution)/shard_map/ppermute | solution.py:594
  12.9 15.9 %collective-permute-start.3 = (f32[2,12,192]{2,1,0:T(8,128)}, f32[2,12,192]{2,1,0:T(8,128)}, u32[]{:S(2)}, u32[]{:S(2)}) collective-permute-start(f32[2,12,192]{2,1,0:T(8,128)} %pack.1), channel_id=1, source_target_pairs={{0,2},{1,3},{2,0},{3,1},{4,6},{5,7},{6,4},{7,5},{8,10},{9,11},{10,... | collective-permute-start | bytes 55304 | tf_op jit(solution)/shard_map/ppermute | solution.py:594
  14.2 26.4 %collective-permute-start.6 = (bf16[96,3072]{1,0:T(8,128)(2,1)S(1)}, bf16[96,3072]{1,0:T(8,128)(2,1)S(1)}, u32[]{:S(2)}, u32[]{:S(2)}) collective-permute-start(bf16[96,3072]{1,0:T(8,128)(2,1)S(1)} %get-tuple-element.424), channel_id=1, source_target_pairs={{0,2},{1,3},{2,0},{3,1},{4,6},{5,7},{6,4},{7,5},{8,10},{9,11},{10,... | collective-permute-start | bytes 1769480 | tf_op jit(solution)/shard_map/ppermute | solution.py:22
  28.7 11.9 %collective-permute-start.5 = (bf16[2,192,768]{2,1,0:T(8,128)(2,1)}, bf16[2,192,768]{2,1,0:T(8,128)(2,1)}, u32[]{:S(2)}, u32[]{:S(2)}) collective-permute-start(bf16[2,192,768]{2,1,0:T(8,128)(2,1)} %rest_2_.7), channel_id=1, source_target_pairs={{0,1},{1,0},{2,3},{3,2},{4,5},{5,4},{6,7},{7,6},{8,9},{9,8},{10,11... | collective-permute-start | bytes 1769480 | tf_op jit(solution)/shard_map/ppermute | solution.py:22
  40.6 20.6 %collective-permute-start.9 = (bf16[2,192,3072]{2,1,0:T(8,128)(2,1)}, bf16[2,192,3072]{2,1,0:T(8,128)(2,1)S(1)}, u32[]{:S(2)}, u32[]{:S(2)}) collective-permute-start(bf16[2,192,3072]{2,1,0:T(8,128)(2,1)} %rest_0_.14), channel_id=1, source_target_pairs={{0,1},{1,0},{2,3},{3,2},{4,5},{5,4},{6,7},{7,6},{8,9},{9,8},{10,11... | collective-permute-start | bytes 7077896 | tf_op jit(solution)/shard_map/ppermute | solution.py:22
  40.6 15.8 %collective-permute-start.2 = (bf16[96,3072]{1,0:T(8,128)(2,1)S(1)}, bf16[96,3072]{1,0:T(8,128)(2,1)S(1)}, u32[]{:S(2)}, u32[]{:S(2)}) collective-permute-start(bf16[96,3072]{1,0:T(8,128)(2,1)S(1)} %collective-permute-done.rest_4_), channel_id=1, source_target_pairs={{0,4},{4,0},{8,12},{12,8},{16,20},{20,16},{24,28},{28,24},{1,5},{5... | collective-permute-start | bytes 1769480 | tf_op jit(solution)/shard_map/ppermute | solution.py:22
  57.2 4.0 collective-permute-start.8
  57.9 15.8 %collective-permute-start.10 = (bf16[384,768]{1,0:T(8,128)(2,1)S(1)}, bf16[384,768]{1,0:T(8,128)(2,1)S(1)}, u32[]{:S(2)}, u32[]{:S(2)}) collective-permute-start(bf16[384,768]{1,0:T(8,128)(2,1)S(1)} %get-tuple-element.452), channel_id=1, source_target_pairs={{0,2},{1,3},{2,0},{3,1},{4,6},{5,7},{6,4},{7,5},{8,10},{9,11},{10,... | collective-permute-start | bytes 1769480 | tf_op jit(solution)/shard_map/ppermute | solution.py:22
  59.7 15.5 %collective-permute-start.13 = (bf16[96,3072]{1,0:T(8,128)(2,1)S(1)}, bf16[96,3072]{1,0:T(8,128)(2,1)S(1)}, u32[]{:S(2)}, u32[]{:S(2)}) collective-permute-start(bf16[96,3072]{1,0:T(8,128)(2,1)S(1)} %collective-permute-done.6.rest_2_), channel_id=1, source_target_pairs={{0,4},{4,0},{8,12},{12,8},{16,20},{20,16},{24,28},{28,24},{1,5},{5... | collective-permute-start | bytes 1769480 | tf_op jit(solution)/shard_map/ppermute | solution.py:22
  62.3 15.8 %collective-permute-start.15 = (bf16[2,768,768]{2,1,0:T(8,128)(2,1)S(1)}, bf16[2,768,768]{2,1,0:T(8,128)(2,1)}, u32[]{:S(2)}, u32[]{:S(2)}) collective-permute-start(bf16[2,768,768]{2,1,0:T(8,128)(2,1)S(1)} %copy-done.7), channel_id=1, source_target_pairs={{0,1},{1,0},{2,3},{3,2},{4,5},{5,4},{6,7},{7,6},{8,9},{9,8},{10,11... | collective-permute-start | bytes 7077896 | tf_op jit(solution)/shard_map/ppermute | solution.py:22
  76.0 15.7 %collective-permute-start.12 = (bf16[96,3072]{1,0:T(8,128)(2,1)S(1)}, bf16[96,3072]{1,0:T(8,128)(2,1)S(1)}, u32[]{:S(2)}, u32[]{:S(2)}) collective-permute-start(bf16[96,3072]{1,0:T(8,128)(2,1)S(1)} %copy-done.19), channel_id=1, source_target_pairs={{0,2},{1,3},{2,0},{3,1},{4,6},{5,7},{6,4},{7,5},{8,10},{9,11},{10,... | collective-permute-start | bytes 1769480 | tf_op jit(solution)/shard_map/ppermute | solution.py:22
  76.5 15.5 %collective-permute-start.11 = (bf16[384,768]{1,0:T(8,128)(2,1)S(1)}, bf16[384,768]{1,0:T(8,128)(2,1)S(1)}, u32[]{:S(2)}, u32[]{:S(2)}) collective-permute-start(bf16[384,768]{1,0:T(8,128)(2,1)S(1)} %collective-permute-done.10.rest_7_), channel_id=1, source_target_pairs={{0,4},{4,0},{8,12},{12,8},{16,20},{20,16},{24,28},{28,24},{1,5},{5... | collective-permute-start | bytes 1769480 | tf_op jit(solution)/shard_map/ppermute | solution.py:22
  92.8 3.1 collective-permute-start.16
  92.8 15.7 %collective-permute-start.18 = (bf16[96,3072]{1,0:T(8,128)(2,1)S(1)}, bf16[96,3072]{1,0:T(8,128)(2,1)S(1)}, u32[]{:S(2)}, u32[]{:S(2)}) collective-permute-start(bf16[96,3072]{1,0:T(8,128)(2,1)S(1)} %get-tuple-element.485), channel_id=1, source_target_pairs={{0,2},{1,3},{2,0},{3,1},{4,6},{5,7},{6,4},{7,5},{8,10},{9,11},{10,... | collective-permute-start | bytes 1769480 | tf_op jit(solution)/shard_map/ppermute | solution.py:22
  94.3 15.5 %collective-permute-start.17 = (bf16[96,3072]{1,0:T(8,128)(2,1)S(1)}, bf16[96,3072]{1,0:T(8,128)(2,1)S(1)}, u32[]{:S(2)}, u32[]{:S(2)}) collective-permute-start(bf16[96,3072]{1,0:T(8,128)(2,1)S(1)} %collective-permute-done.12.rest_4_), channel_id=1, source_target_pairs={{0,4},{4,0},{8,12},{12,8},{16,20},{20,16},{24,28},{28,24},{1,5},{5... | collective-permute-start | bytes 1769480 | tf_op jit(solution)/shard_map/ppermute | solution.py:22
  110.6 16.2 %collective-permute-start.20 = (bf16[384,768]{1,0:T(8,128)(2,1)S(1)}, bf16[384,768]{1,0:T(8,128)(2,1)S(1)}, u32[]{:S(2)}, u32[]{:S(2)}) collective-permute-start(bf16[384,768]{1,0:T(8,128)(2,1)S(1)} %get-tuple-element.498), channel_id=1, source_target_pairs={{0,2},{1,3},{2,0},{3,1},{4,6},{5,7},{6,4},{7,5},{8,10},{9,11},{10,... | collective-permute-start | bytes 1769480 | tf_op jit(solution)/shard_map/ppermute | solution.py:22
  111.5 16.8 %collective-permute-start.22 = (bf16[96,3072]{1,0:T(8,128)(2,1)S(1)}, bf16[96,3072]{1,0:T(8,128)(2,1)S(1)}, u32[]{:S(2)}, u32[]{:S(2)}) collective-permute-start(bf16[96,3072]{1,0:T(8,128)(2,1)S(1)} %collective-permute-done.18.rest_2_), channel_id=1, source_target_pairs={{0,4},{4,0},{8,12},{12,8},{16,20},{20,16},{24,28},{28,24},{1,5},{5... | collective-permute-start | bytes 1769480 | tf_op jit(solution)/shard_map/ppermute | solution.py:22
  126.8 15.0 %collective-permute-start.21 = (bf16[384,768]{1,0:T(8,128)(2,1)S(1)}, bf16[384,768]{1,0:T(8,128)(2,1)S(1)}, u32[]{:S(2)}, u32[]{:S(2)}) collective-permute-start(bf16[384,768]{1,0:T(8,128)(2,1)S(1)} %collective-permute-done.20.rest_7_), channel_id=1, source_target_pairs={{0,4},{4,0},{8,12},{12,8},{16,20},{20,16},{24,28},{28,24},{1,5},{5... | collective-permute-start | bytes 1769480 | tf_op jit(solution)/shard_map/ppermute | solution.py:22
  129.1 13.5 %collective-permute-start.24 = (bf16[192,3072]{1,0:T(8,128)(2,1)S(1)}, bf16[192,3072]{1,0:T(8,128)(2,1)S(1)}, u32[]{:S(2)}, u32[]{:S(2)}) collective-permute-start(bf16[192,3072]{1,0:T(8,128)(2,1)S(1)} %pad_maximum_fusion.4), channel_id=1, source_target_pairs={{0,1},{1,0},{2,3},{3,2},{4,5},{5,4},{6,7},{7,6},{8,9},{9,8},{10,11... | collective-permute-start | bytes 3538952 | tf_op jit(solution)/shard_map/ppermute | solution.py:22
  163.2 13.8 %collective-permute-start.26 = (bf16[2,2,2,2,192,384]{5,4,3,2,1,0:T(8,128)(2,1)}, bf16[2,2,2,2,192,384]{5,4,3,2,1,0:T(8,128)(2,1)S(1)}, u32[]{:S(2)}, u32[]{:S(2)}) collective-permute-start(bf16[2,2,2,2,192,384]{5,4,3,2,1,0:T(8,128)(2,1)} %get-tuple-element.536), channel_id=1, source_target_pairs={{0,1},{1,0},{2,3},{3,2},{4,5},{5,4},{6,7},{7,6},{8,9},{9,8},{10,11... | collective-permute-start | bytes 7077896 | tf_op jit(solution)/shard_map/ppermute | solution.py:22
  176.6 4.8 %collective-permute-start.25 = (bf16[2,2,2,2,192,384]{5,4,3,2,1,0:T(8,128)(2,1)}, bf16[2,2,2,2,192,384]{5,4,3,2,1,0:T(8,128)(2,1)S(1)}, u32[]{:S(2)}, u32[]{:S(2)}) collective-permute-start(bf16[2,2,2,2,192,384]{5,4,3,2,1,0:T(8,128)(2,1)} %get-tuple-element.534), channel_id=1, source_target_pairs={{0,1},{1,0},{2,3},{3,2},{4,5},{5,4},{6,7},{7,6},{8,9},{9,8},{10,11... | collective-permute-start | bytes 7077896 | tf_op jit(solution)/shard_map/ppermute | solution.py:22
  195.1 36.8 %collective-permute-start.31 = (bf16[2,2,2,2,192,384]{5,4,3,2,1,0:T(8,128)(2,1)}, bf16[2,2,2,2,192,384]{5,4,3,2,1,0:T(8,128)(2,1)S(1)}, u32[]{:S(2)}, u32[]{:S(2)}) collective-permute-start(bf16[2,2,2,2,192,384]{5,4,3,2,1,0:T(8,128)(2,1)} %get-tuple-element.566), channel_id=1, source_target_pairs={{0,1},{1,0},{2,3},{3,2},{4,5},{5,4},{6,7},{7,6},{8,9},{9,8},{10,11... | collective-permute-start | bytes 7077896 | tf_op jit(solution)/shard_map/ppermute | solution.py:22
  201.6 31.8 %collective-permute-start.29 = (bf16[2,2,2,2,192,384]{5,4,3,2,1,0:T(8,128)(2,1)}, bf16[2,2,2,2,192,384]{5,4,3,2,1,0:T(8,128)(2,1)S(1)}, u32[]{:S(2)}, u32[]{:S(2)}) collective-permute-start(bf16[2,2,2,2,192,384]{5,4,3,2,1,0:T(8,128)(2,1)} %get-tuple-element.563), channel_id=1, source_target_pairs={{0,1},{1,0},{2,3},{3,2},{4,5},{5,4},{6,7},{7,6},{8,9},{9,8},{10,11... | collective-permute-start | bytes 7077896 | tf_op jit(solution)/shard_map/ppermute | solution.py:22
  201.8 28.3 %collective-permute-start.27 = (bf16[2,2,2,192,384]{4,3,2,1,0:T(8,128)(2,1)S(1)}, bf16[2,2,2,192,384]{4,3,2,1,0:T(8,128)(2,1)S(1)}, u32[]{:S(2)}, u32[]{:S(2)}) collective-permute-start(bf16[2,2,2,192,384]{4,3,2,1,0:T(8,128)(2,1)S(1)} %get-tuple-element.557), channel_id=1, source_target_pairs={{0,2},{1,3},{2,0},{3,1},{4,6},{5,7},{6,4},{7,5},{8,10},{9,11},{10,... | collective-permute-start | bytes 3538952 | tf_op jit(solution)/shard_map/ppermute | solution.py:22
  202.2 30.4 %collective-permute-start.30 = (bf16[2,2,2,192,384]{4,3,2,1,0:T(8,128)(2,1)S(1)}, bf16[2,2,2,192,384]{4,3,2,1,0:T(8,128)(2,1)S(1)}, u32[]{:S(2)}, u32[]{:S(2)}) collective-permute-start(bf16[2,2,2,192,384]{4,3,2,1,0:T(8,128)(2,1)S(1)} %get-tuple-element.564), channel_id=1, source_target_pairs={{0,8},{4,12},{8,0},{12,4},{16,24},{20,28},{24,16},{28,20},{1,9},{5... | collective-permute-start | bytes 3538952 | tf_op jit(solution)/shard_map/ppermute | solution.py:22
  230.4 14.9 %collective-permute-start.28 = (bf16[2,2,192,384]{3,2,1,0:T(8,128)(2,1)S(1)}, bf16[2,2,192,384]{3,2,1,0:T(8,128)(2,1)S(1)}, u32[]{:S(2)}, u32[]{:S(2)}) collective-permute-start(bf16[2,2,192,384]{3,2,1,0:T(8,128)(2,1)S(1)} %get-tuple-element.561), channel_id=1, source_target_pairs={{0,4},{4,0},{8,12},{12,8},{16,20},{20,16},{24,28},{28,24},{1,5},{5... | collective-permute-start | bytes 1769480 | tf_op jit(solution)/shard_map/ppermute | solution.py:22
  232.9 14.7 %collective-permute-start.33 = (bf16[2,2,192,384]{3,2,1,0:T(8,128)(2,1)S(1)}, bf16[2,2,192,384]{3,2,1,0:T(8,128)(2,1)S(1)}, u32[]{:S(2)}, u32[]{:S(2)}) collective-permute-start(bf16[2,2,192,384]{3,2,1,0:T(8,128)(2,1)S(1)} %get-tuple-element.580), channel_id=1, source_target_pairs={{0,2},{1,3},{2,0},{3,1},{4,6},{5,7},{6,4},{7,5},{8,10},{9,11},{10,... | collective-permute-start | bytes 1769480 | tf_op jit(solution)/shard_map/ppermute | solution.py:22
  245.4 7.7 %collective-permute-start.32 = (bf16[2,192,384]{2,1,0:T(8,128)(2,1)S(1)}, bf16[2,192,384]{2,1,0:T(8,128)(2,1)S(1)}, u32[]{:S(2)}, u32[]{:S(2)}) collective-permute-start(bf16[2,192,384]{2,1,0:T(8,128)(2,1)S(1)} %fusion.51), channel_id=1, source_target_pairs={{0,8},{4,12},{8,0},{12,4},{16,24},{20,28},{24,16},{28,20},{1,9},{5... | collective-permute-start | bytes 884744 | tf_op jit(solution)/shard_map/ppermute | solution.py:22
  266.0 31.6 %collective-permute-start.39 = (bf16[2,2,2,2,192,384]{5,4,3,2,1,0:T(8,128)(2,1)}, bf16[2,2,2,2,192,384]{5,4,3,2,1,0:T(8,128)(2,1)S(1)}, u32[]{:S(2)}, u32[]{:S(2)}) collective-permute-start(bf16[2,2,2,2,192,384]{5,4,3,2,1,0:T(8,128)(2,1)} %get-tuple-element.607), channel_id=1, source_target_pairs={{0,1},{1,0},{2,3},{3,2},{4,5},{5,4},{6,7},{7,6},{8,9},{9,8},{10,11... | collective-permute-start | bytes 7077896 | tf_op jit(solution)/shard_map/ppermute | solution.py:22
  266.1 28.8 %collective-permute-start.36 = (bf16[2,2,2,192,384]{4,3,2,1,0:T(8,128)(2,1)S(1)}, bf16[2,2,2,192,384]{4,3,2,1,0:T(8,128)(2,1)S(1)}, u32[]{:S(2)}, u32[]{:S(2)}) collective-permute-start(bf16[2,2,2,192,384]{4,3,2,1,0:T(8,128)(2,1)S(1)} %get-tuple-element.597), channel_id=1, source_target_pairs={{0,4},{4,0},{8,12},{12,8},{16,20},{20,16},{24,28},{28,24},{1,5},{5... | collective-permute-start | bytes 3538952 | tf_op jit(solution)/shard_map/ppermute | solution.py:22
  267.6 28.5 %collective-permute-start.35 = (bf16[2,192,384]{2,1,0:T(8,128)(2,1)S(1)}, bf16[2,192,384]{2,1,0:T(8,128)(2,1)S(1)}, u32[]{:S(2)}, u32[]{:S(2)}) collective-permute-start(bf16[2,192,384]{2,1,0:T(8,128)(2,1)S(1)} %fusion.40), channel_id=1, source_target_pairs={{0,16},{4,20},{8,24},{12,28},{16,0},{20,4},{24,8},{28,12},{1,17},{... | collective-permute-start | bytes 884744 | tf_op jit(solution)/shard_map/ppermute | solution.py:22
  270.1 34.3 %collective-permute-start.34 = (bf16[2,2,2,192,384]{4,3,2,1,0:T(8,128)(2,1)S(1)}, bf16[2,2,2,192,384]{4,3,2,1,0:T(8,128)(2,1)S(1)}, u32[]{:S(2)}, u32[]{:S(2)}) collective-permute-start(bf16[2,2,2,192,384]{4,3,2,1,0:T(8,128)(2,1)S(1)} %get-tuple-element.595), channel_id=1, source_target_pairs={{0,2},{1,3},{2,0},{3,1},{4,6},{5,7},{6,4},{7,5},{8,10},{9,11},{10,... | collective-permute-start | bytes 3538952 | tf_op jit(solution)/shard_map/ppermute | solution.py:22
  270.6 30.3 %collective-permute-start.38 = (bf16[2,192,384]{2,1,0:T(8,128)(2,1)S(1)}, bf16[2,192,384]{2,1,0:T(8,128)(2,1)S(1)}, u32[]{:S(2)}, u32[]{:S(2)}) collective-permute-start(bf16[2,192,384]{2,1,0:T(8,128)(2,1)S(1)} %fusion.52), channel_id=1, source_target_pairs={{0,4},{4,0},{8,12},{12,8},{16,20},{20,16},{24,28},{28,24},{1,5},{5... | collective-permute-start | bytes 884744 | tf_op jit(solution)/shard_map/ppermute | solution.py:22
  296.2 8.2 %collective-permute-start.37 = (bf16[1,2,192,384]{3,2,1,0:T(8,128)(2,1)S(1)}, bf16[1,2,192,384]{3,2,1,0:T(8,128)(2,1)S(1)}, u32[]{:S(2)}, u32[]{:S(2)}) collective-permute-start(bf16[1,2,192,384]{3,2,1,0:T(8,128)(2,1)S(1)} %fusion.45), channel_id=1, source_target_pairs={{0,8},{4,12},{8,0},{12,4},{16,24},{20,28},{24,16},{28,20},{1,9},{5... | collective-permute-start | bytes 884744 | tf_op jit(solution)/shard_map/ppermute | solution.py:22
  318.5 24.0 %collective-permute-start.40 = (bf16[2,2,2,2,208,384]{5,4,3,2,1,0:T(8,128)(2,1)}, bf16[2,2,2,2,208,384]{5,4,3,2,1,0:T(8,128)(2,1)S(1)}, u32[]{:S(2)}, u32[]{:S(2)}) collective-permute-start(bf16[2,2,2,2,208,384]{5,4,3,2,1,0:T(8,128)(2,1)} %get-tuple-element.636), channel_id=1, source_target_pairs={{0,1},{1,0},{2,3},{3,2},{4,5},{5,4},{6,7},{7,6},{8,9},{9,8},{10,11... | collective-permute-start | bytes 7667720 | tf_op jit(solution)/shard_map/ppermute | solution.py:22
  318.6 15.7 %collective-permute-start.43 = (bf16[2,2,192,384]{3,2,1,0:T(8,128)(2,1)S(1)}, bf16[2,2,192,384]{3,2,1,0:T(8,128)(2,1)S(1)}, u32[]{:S(2)}, u32[]{:S(2)}) collective-permute-start(bf16[2,2,192,384]{3,2,1,0:T(8,128)(2,1)S(1)} %pad_maximum_fusion.9.near), channel_id=1, source_target_pairs={{0,4},{4,0},{8,12},{12,8},{16,20},{20,16},{24,28},{28,24},{1,5},{5... | collective-permute-start | bytes 1769480 | tf_op jit(solution)/shard_map/ppermute | solution.py:22
  320.0 19.2 %collective-permute-start.42 = (bf16[2,2,192,384]{3,2,1,0:T(8,128)(2,1)}, bf16[2,2,192,384]{3,2,1,0:T(8,128)(2,1)}, u32[]{:S(2)}, u32[]{:S(2)}) collective-permute-start(bf16[2,2,192,384]{3,2,1,0:T(8,128)(2,1)} %get-tuple-element.638), channel_id=1, source_target_pairs={{0,2},{1,3},{2,0},{3,1},{4,6},{5,7},{6,4},{7,5},{8,10},{9,11},{10,... | collective-permute-start | bytes 1769480 | tf_op jit(solution)/shard_map/ppermute | solution.py:22
  320.4 19.9 %collective-permute-start.41 = (bf16[2,192,384]{2,1,0:T(8,128)(2,1)S(1)}, bf16[2,192,384]{2,1,0:T(8,128)(2,1)S(1)}, u32[]{:S(2)}, u32[]{:S(2)}) collective-permute-start(bf16[2,192,384]{2,1,0:T(8,128)(2,1)S(1)} %fusion.36), channel_id=1, source_target_pairs={{0,16},{4,20},{8,24},{12,28},{16,0},{20,4},{24,8},{28,12},{1,17},{... | collective-permute-start | bytes 884744 | tf_op jit(solution)/shard_map/ppermute | solution.py:22
  323.0 20.9 %collective-permute-start.46 = (bf16[2,2,192,384]{3,2,1,0:T(8,128)(2,1)}, bf16[2,2,192,384]{3,2,1,0:T(8,128)(2,1)}, u32[]{:S(2)}, u32[]{:S(2)}) collective-permute-start(bf16[2,2,192,384]{3,2,1,0:T(8,128)(2,1)} %get-tuple-element.658), channel_id=1, source_target_pairs={{0,8},{4,12},{8,0},{12,4},{16,24},{20,28},{24,16},{28,20},{1,9},{5... | collective-permute-start | bytes 1769480 | tf_op jit(solution)/shard_map/ppermute | solution.py:22
  335.2 27.9 %collective-permute-start.48 = (bf16[2,2,2,192,384]{4,3,2,1,0:T(8,128)(2,1)}, bf16[2,2,2,192,384]{4,3,2,1,0:T(8,128)(2,1)}, u32[]{:S(2)}, u32[]{:S(2)}) collective-permute-start(bf16[2,2,2,192,384]{4,3,2,1,0:T(8,128)(2,1)} %get-tuple-element.666), channel_id=1, source_target_pairs={{0,2},{1,3},{2,0},{3,1},{4,6},{5,7},{6,4},{7,5},{8,10},{9,11},{10,... | collective-permute-start | bytes 3538952 | tf_op jit(solution)/shard_map/ppermute | solution.py:22
  340.4 26.6 %collective-permute-start.51 = (bf16[1,2,192,384]{3,2,1,0:T(8,128)(2,1)S(1)}, bf16[1,2,192,384]{3,2,1,0:T(8,128)(2,1)S(1)}, u32[]{:S(2)}, u32[]{:S(2)}) collective-permute-start(bf16[1,2,192,384]{3,2,1,0:T(8,128)(2,1)S(1)} %fusion.46), channel_id=1, source_target_pairs={{0,8},{4,12},{8,0},{12,4},{16,24},{20,28},{24,16},{28,20},{1,9},{5... | collective-permute-start | bytes 884744 | tf_op jit(solution)/shard_map/ppermute | solution.py:22
  342.1 13.8 %collective-permute-start.45 = (bf16[2,192,384]{2,1,0:T(8,128)(2,1)S(1)}, bf16[2,192,384]{2,1,0:T(8,128)(2,1)S(1)}, u32[]{:S(2)}, u32[]{:S(2)}) collective-permute-start(bf16[2,192,384]{2,1,0:T(8,128)(2,1)S(1)} %fusion.54), channel_id=1, source_target_pairs={{0,8},{4,12},{8,0},{12,4},{16,24},{20,28},{24,16},{28,20},{1,9},{5... | collective-permute-start | bytes 884744 | tf_op jit(solution)/shard_map/ppermute | solution.py:22
  363.1 30.5 %collective-permute-start.44 = (bf16[2,2,2,208,384]{4,3,2,1,0:T(8,128)(2,1)S(1)}, bf16[2,2,2,208,384]{4,3,2,1,0:T(8,128)(2,1)S(1)}, u32[]{:S(2)}, u32[]{:S(2)}) collective-permute-start(bf16[2,2,2,208,384]{4,3,2,1,0:T(8,128)(2,1)S(1)} %get-tuple-element.656), channel_id=1, source_target_pairs={{0,2},{1,3},{2,0},{3,1},{4,6},{5,7},{6,4},{7,5},{8,10},{9,11},{10,... | collective-permute-start | bytes 3833864 | tf_op jit(solution)/shard_map/ppermute | solution.py:22
  364.9 26.4 %collective-permute-start.49 = (bf16[2,2,192,384]{3,2,1,0:T(8,128)(2,1)S(1)}, bf16[2,2,192,384]{3,2,1,0:T(8,128)(2,1)S(1)}, u32[]{:S(2)}, u32[]{:S(2)}) collective-permute-start(bf16[2,2,192,384]{3,2,1,0:T(8,128)(2,1)S(1)} %get-tuple-element.670), channel_id=1, source_target_pairs={{0,4},{4,0},{8,12},{12,8},{16,20},{20,16},{24,28},{28,24},{1,5},{5... | collective-permute-start | bytes 1769480 | tf_op jit(solution)/shard_map/ppermute | solution.py:22
  366.5 21.1 %collective-permute-start.50 = (bf16[2,192,384]{2,1,0:T(8,128)(2,1)S(1)}, bf16[2,192,384]{2,1,0:T(8,128)(2,1)S(1)}, u32[]{:S(2)}, u32[]{:S(2)}) collective-permute-start(bf16[2,192,384]{2,1,0:T(8,128)(2,1)S(1)} %fusion.56), channel_id=1, source_target_pairs={{0,4},{4,0},{8,12},{12,8},{16,20},{20,16},{24,28},{28,24},{1,5},{5... | collective-permute-start | bytes 884744 | tf_op jit(solution)/shard_map/ppermute | solution.py:22
  367.1 24.3 %collective-permute-start.47 = (bf16[2,192,384]{2,1,0:T(8,128)(2,1)S(1)}, bf16[2,192,384]{2,1,0:T(8,128)(2,1)S(1)}, u32[]{:S(2)}, u32[]{:S(2)}) collective-permute-start(bf16[2,192,384]{2,1,0:T(8,128)(2,1)S(1)} %fusion.33), channel_id=1, source_target_pairs={{0,16},{4,20},{8,24},{12,28},{16,0},{20,4},{24,8},{28,12},{1,17},{... | collective-permute-start | bytes 884744 | tf_op jit(solution)/shard_map/ppermute | solution.py:22
  369.7 38.9 %collective-permute-start.54 = (bf16[2,2,192,384]{3,2,1,0:T(8,128)(2,1)S(1)}, bf16[2,2,192,384]{3,2,1,0:T(8,128)(2,1)S(1)}, u32[]{:S(2)}, u32[]{:S(2)}) collective-permute-start(bf16[2,2,192,384]{3,2,1,0:T(8,128)(2,1)S(1)} %pad_maximum_fusion.10.near), channel_id=1, source_target_pairs={{0,4},{4,0},{8,12},{12,8},{16,20},{20,16},{24,28},{28,24},{1,5},{5... | collective-permute-start | bytes 1769480 | tf_op jit(solution)/shard_map/ppermute | solution.py:22
  388.6 18.5 %collective-permute-start.55 = (bf16[2,192,384]{2,1,0:T(8,128)(2,1)S(1)}, bf16[2,192,384]{2,1,0:T(8,128)(2,1)S(1)}, u32[]{:S(2)}, u32[]{:S(2)}) collective-permute-start(bf16[2,192,384]{2,1,0:T(8,128)(2,1)S(1)} %fusion.29), channel_id=1, source_target_pairs={{0,16},{4,20},{8,24},{12,28},{16,0},{20,4},{24,8},{28,12},{1,17},{... | collective-permute-start | bytes 884744 | tf_op jit(solution)/shard_map/ppermute | solution.py:22
  391.4 15.7 %collective-permute-start.56 = (bf16[2,192,384]{2,1,0:T(8,128)(2,1)S(1)}, bf16[2,192,384]{2,1,0:T(8,128)(2,1)S(1)}, u32[]{:S(2)}, u32[]{:S(2)}) collective-permute-start(bf16[2,192,384]{2,1,0:T(8,128)(2,1)S(1)} %fusion.57), channel_id=1, source_target_pairs={{0,8},{4,12},{8,0},{12,4},{16,24},{20,28},{24,16},{28,20},{1,9},{5... | collective-permute-start | bytes 884744 | tf_op jit(solution)/shard_map/ppermute | solution.py:22
  393.1 23.1 %collective-permute-start.53 = (bf16[1,2,192,384]{3,2,1,0:T(8,128)(2,1)S(1)}, bf16[1,2,192,384]{3,2,1,0:T(8,128)(2,1)S(1)}, u32[]{:S(2)}, u32[]{:S(2)}) collective-permute-start(bf16[1,2,192,384]{3,2,1,0:T(8,128)(2,1)S(1)} %fusion.47), channel_id=1, source_target_pairs={{0,8},{4,12},{8,0},{12,4},{16,24},{20,28},{24,16},{28,20},{1,9},{5... | collective-permute-start | bytes 884744 | tf_op jit(solution)/shard_map/ppermute | solution.py:22
  407.2 17.3 %collective-permute-start.52 = (bf16[2,2,208,384]{3,2,1,0:T(8,128)(2,1)S(1)}, bf16[2,2,208,384]{3,2,1,0:T(8,128)(2,1)S(1)}, u32[]{:S(2)}, u32[]{:S(2)}) collective-permute-start(bf16[2,2,208,384]{3,2,1,0:T(8,128)(2,1)S(1)} %get-tuple-element.688), channel_id=1, source_target_pairs={{0,4},{4,0},{8,12},{12,8},{16,20},{20,16},{24,28},{28,24},{1,5},{5... | collective-permute-start | bytes 1916936 | tf_op jit(solution)/shard_map/ppermute | solution.py:22
  408.6 16.0 %collective-permute-start.59 = (bf16[1,2,192,384]{3,2,1,0:T(8,128)(2,1)S(1)}, bf16[1,2,192,384]{3,2,1,0:T(8,128)(2,1)S(1)}, u32[]{:S(2)}, u32[]{:S(2)}) collective-permute-start(bf16[1,2,192,384]{3,2,1,0:T(8,128)(2,1)S(1)} %fusion.48), channel_id=1, source_target_pairs={{0,8},{4,12},{8,0},{12,4},{16,24},{20,28},{24,16},{28,20},{1,9},{5... | collective-permute-start | bytes 884744 | tf_op jit(solution)/shard_map/ppermute | solution.py:22
  409.4 15.9 %collective-permute-start.58 = (bf16[2,192,384]{2,1,0:T(8,128)(2,1)S(1)}, bf16[2,192,384]{2,1,0:T(8,128)(2,1)S(1)}, u32[]{:S(2)}, u32[]{:S(2)}) collective-permute-start(bf16[2,192,384]{2,1,0:T(8,128)(2,1)S(1)} %fusion.27), channel_id=1, source_target_pairs={{0,16},{4,20},{8,24},{12,28},{16,0},{20,4},{24,8},{28,12},{1,17},{... | collective-permute-start | bytes 884744 | tf_op jit(solution)/shard_map/ppermute | solution.py:22
  416.3 20.9 %collective-permute-start.62 = (bf16[2,2,192,384]{3,2,1,0:T(8,128)(2,1)S(1)}, bf16[2,2,192,384]{3,2,1,0:T(8,128)(2,1)S(1)}, u32[]{:S(2)}, u32[]{:S(2)}) collective-permute-start(bf16[2,2,192,384]{3,2,1,0:T(8,128)(2,1)S(1)} %pad_maximum_fusion.11.near), channel_id=1, source_target_pairs={{0,4},{4,0},{8,12},{12,8},{16,20},{20,16},{24,28},{28,24},{1,5},{5... | collective-permute-start | bytes 1769480 | tf_op jit(solution)/shard_map/ppermute | solution.py:22
  424.6 10.4 %collective-permute-start.57 = (bf16[2,208,384]{2,1,0:T(8,128)(2,1)S(1)}, bf16[2,208,384]{2,1,0:T(8,128)(2,1)S(1)}, u32[]{:S(2)}, u32[]{:S(2)}) collective-permute-start(bf16[2,208,384]{2,1,0:T(8,128)(2,1)S(1)} %fusion.44), channel_id=1, source_target_pairs={{0,8},{4,12},{8,0},{12,4},{16,24},{20,28},{24,16},{28,20},{1,9},{5... | collective-permute-start | bytes 958472 | tf_op jit(solution)/shard_map/ppermute | solution.py:22
  425.4 27.4 %collective-permute-start.64 = (bf16[1,2,192,384]{3,2,1,0:T(8,128)(2,1)S(1)}, bf16[1,2,192,384]{3,2,1,0:T(8,128)(2,1)S(1)}, u32[]{:S(2)}, u32[]{:S(2)}) collective-permute-start(bf16[1,2,192,384]{3,2,1,0:T(8,128)(2,1)S(1)} %fusion.49), channel_id=1, source_target_pairs={{0,4},{4,0},{8,12},{12,8},{16,20},{20,16},{24,28},{28,24},{1,5},{5... | collective-permute-start | bytes 884744 | tf_op jit(solution)/shard_map/ppermute | solution.py:22
  427.0 21.2 %collective-permute-start.61 = (bf16[2,2,192,384]{3,2,1,0:T(8,128)(2,1)S(1)}, bf16[2,2,192,384]{3,2,1,0:T(8,128)(2,1)S(1)}, u32[]{:S(2)}, u32[]{:S(2)}) collective-permute-start(bf16[2,2,192,384]{3,2,1,0:T(8,128)(2,1)S(1)} %pad_maximum_fusion.12.near), channel_id=1, source_target_pairs={{0,4},{4,0},{8,12},{12,8},{16,20},{20,16},{24,28},{28,24},{1,5},{5... | collective-permute-start | bytes 1769480 | tf_op jit(solution)/shard_map/ppermute | solution.py:22
  435.1 17.6 %collective-permute-start.60 = (bf16[2,208,384]{2,1,0:T(8,128)(2,1)S(1)}, bf16[2,208,384]{2,1,0:T(8,128)(2,1)S(1)}, u32[]{:S(2)}, u32[]{:S(2)}) collective-permute-start(bf16[2,208,384]{2,1,0:T(8,128)(2,1)S(1)} %fusion.20), channel_id=1, source_target_pairs={{0,16},{4,20},{8,24},{12,28},{16,0},{20,4},{24,8},{28,12},{1,17},{... | collective-permute-start | bytes 958472 | tf_op jit(solution)/shard_map/ppermute | solution.py:22
  452.8 8.0 %collective-permute-start.63 = (bf16[1,2,208,384]{3,2,1,0:T(8,128)(2,1)S(1)}, bf16[1,2,208,384]{3,2,1,0:T(8,128)(2,1)S(1)}, u32[]{:S(2)}, u32[]{:S(2)}) collective-permute-start(bf16[1,2,208,384]{3,2,1,0:T(8,128)(2,1)S(1)} %fusion.42), channel_id=1, source_target_pairs={{0,8},{4,12},{8,0},{12,4},{16,24},{20,28},{24,16},{28,20},{1,9},{5... | collective-permute-start | bytes 958472 | tf_op jit(solution)/shard_map/ppermute | solution.py:22
  453.0 14.1 %collective-permute-start.66 = (bf16[2,2,192,384]{3,2,1,0:T(8,128)(2,1)S(1)}, bf16[2,2,192,384]{3,2,1,0:T(8,128)(2,1)S(1)}, u32[]{:S(2)}, u32[]{:S(2)}) collective-permute-start(bf16[2,2,192,384]{3,2,1,0:T(8,128)(2,1)S(1)} %pad_maximum_fusion.13.near), channel_id=1, source_target_pairs={{0,8},{4,12},{8,0},{12,4},{16,24},{20,28},{24,16},{28,20},{1,9},{5... | collective-permute-start | bytes 1769480 | tf_op jit(solution)/shard_map/ppermute | solution.py:22
  460.9 10.8 %collective-permute-start.65 = (bf16[2,2,208,384]{3,2,1,0:T(8,128)(2,1)S(1)}, bf16[2,2,208,384]{3,2,1,0:T(8,128)(2,1)S(1)}, u32[]{:S(2)}, u32[]{:S(2)}) collective-permute-start(bf16[2,2,208,384]{3,2,1,0:T(8,128)(2,1)S(1)} %pad_maximum_fusion.6.near), channel_id=1, source_target_pairs={{0,4},{4,0},{8,12},{12,8},{16,20},{20,16},{24,28},{28,24},{1,5},{5... | collective-permute-start | bytes 1916936 | tf_op jit(solution)/shard_map/ppermute | solution.py:22
  (43 other events, 340.7 us)
